TPU v7x, 128 devices: a whole 4x4x4 slice. The times are simulated.
128 devices in a mesh: dp: 16 (over y, x), mp: 8 (over z, core).
Axes of the slice: x: 4, y: 4, z: 4, core: 2. Of those that a mesh axis runs over, the one named last changes fastest.
Arguments:
- inputs: bfloat16 [2, 2048, 2048], P(None, 'dp', 'mp'), may hold values from -6 to 6
- cotangent: bfloat16 [2, 2048, 2048], P(None, 'dp', 'mp'), may hold values from -6 to 6
- row_split: int32 [2], replicated, may hold values from 512 to 1536
- first_gain: bfloat16 [2048], P('mp'), may hold values from 0.5 to 1.5
- branch_weight: bfloat16 [2048, 2816], P('dp', 'mp'), may hold values from -0.125 to 0.125
- value_weight: bfloat16 [2048, 2816], P('dp', 'mp'), may hold values from -0.125 to 0.125
- conv_weight: bfloat16 [4, 16, 176], P(None, 'mp'), may hold values from -3 to 3
- conv_bias: bfloat16 [16, 176], P('mp'), may hold values from -2 to 2
- rate_blocks: bfloat16 [16, 176, 176], P('mp'), may hold values from -0.4375 to 0.4375
- input_blocks: bfloat16 [16, 176, 176], P('mp'), may hold values from -0.4375 to 0.4375
- rate_bias: bfloat16 [16, 176], P('mp'), may hold values from -4 to 4
- input_bias: bfloat16 [16, 176], P('mp'), may hold values from -4 to 4
- decay_param: bfloat16 [16, 176], P('mp'), may hold values from -13 to -4
- out_weight: bfloat16 [2816, 2048], P('mp', 'dp'), may hold values from -0.3125 to 0.3125
- second_gain: bfloat16 [2048], P('mp'), may hold values from 0.5 to 1.5
- gate_weight: bfloat16 [2048, 6144], P('dp', 'mp'), may hold values from -0.125 to 0.125
- up_weight: bfloat16 [2048, 6144], P('dp', 'mp'), may hold values from -0.125 to 0.125
- down_weight: bfloat16 [6144, 2048], P('mp', 'dp'), may hold values from -0.15625 to 0.15625
Outputs:
- layer_out: bfloat16 [2, 2048, 2048], P(None, 'dp', 'mp')
- input_grad: float32 [2, 2048, 2048], P(None, 'dp', 'mp')
- first_gain_grad: float32 [2048], P(('mp', 'dp'))
- branch_weight_grad: float32 [2048, 2816], P('dp', 'mp')
- value_weight_grad: float32 [2048, 2816], P('dp', 'mp')
- conv_weight_grad: float32 [4, 16, 176], P(None, 'mp', 'dp')
- conv_bias_grad: float32 [16, 176], P('mp', 'dp')
- rate_blocks_grad: float32 [16, 176, 176], P('mp', 'dp')
- input_blocks_grad: float32 [16, 176, 176], P('mp', 'dp')
- rate_bias_grad: float32 [16, 176], P('mp', 'dp')
- input_bias_grad: float32 [16, 176], P('mp', 'dp')
- decay_param_grad: float32 [16, 176], P('mp', 'dp')
- out_weight_grad: float32 [2816, 2048], P('mp', 'dp')
- second_gain_grad: float32 [2048], P(('mp', 'dp'))
- gate_weight_grad: float32 [2048, 6144], P('dp', 'mp')
- up_weight_grad: float32 [2048, 6144], P('dp', 'mp')
- down_weight_grad: float32 [6144, 2048], P('mp', 'dp')
Inputs may be any that keep to these rules, and one draw needn't show every extreme that they name: row_split leaves each of a micro-batch's two rows at least 1024 tokens, or a quarter of 2048 where that is less.
All inputs are finite; a program needn't handle non-finite values.
Results may differ from a plain program's by a relative error of at most 0.02.
Values may be sent and summed in bfloat16 or wider, within the bound.
No kernel may reach another device: no remote copies, remote signals or barrier semaphores. Data moves between devices by JAX's collectives and lax.ppermute only.
A program may use at most 192 MiB of HBM per device.

v0:
```python
import jax
import jax.numpy as jnp
from jax import lax
from jax.sharding import PartitionSpec as P

EPS = 1e-06


def passed_along(shard, axis, by):
    peers = lax.axis_size(axis)
    pairs = [(i, i + by) for i in range(peers) if 0 <= i + by < peers]
    return lax.ppermute(shard, axis, pairs)


def carried_in(value, axis, join, neutral, backward):
    count, mine = (lax.axis_size(axis), lax.axis_index(axis))
    pieces = jax.tree.map(lambda part: lax.all_gather(part, axis), value)
    if backward:
        pieces = jax.tree.map(lambda part: part[::-1], pieces)
        mine = count - 1 - mine
    so_far = jax.tree.map(
        lambda part, zero: jnp.full_like(part, 0) + jnp.asarray(zero, part.dtype), value, neutral
    )

    def step(position, so_far):
        longer = join(so_far, jax.tree.map(lambda part: part[position], pieces))
        return jax.tree.map(lambda new, old: jnp.where(position < mine, new, old), longer, so_far)

    return lax.fori_loop(0, count - 1, step, so_far)


def link(earlier, later):
    return (earlier[0] * later[0], later[0] * earlier[1] + later[1])


def row_masks(places, split_at, conv_span):
    conv_masks = []
    for conv_step in range(conv_span):
        back_pos = places - conv_step
        same_row = ((back_pos >= split_at) == (places >= split_at)) & (back_pos >= 0)
        conv_masks.append(same_row.astype(jnp.float32)[:, None])
    return conv_masks


def convolve(extended, weight, bias_row, conv_masks):
    conv_span = weight.shape[0]
    tok_count = extended.shape[0] - conv_span + 1
    running = jnp.zeros((tok_count, weight.shape[1]), jnp.float32) + bias_row
    for conv_step in range(conv_span):
        offset = conv_span - 1 - conv_step
        running = (
            running
            + weight[conv_step] * extended[offset : offset + tok_count] * conv_masks[conv_step]
        )
    return running


def gate_terms(rate_pre, input_pre, conv_out, decay_row, keep_mask):
    rate_gate = jax.nn.sigmoid(rate_pre)
    input_gate = jax.nn.sigmoid(input_pre)
    log_decay = -8.0 * jax.nn.softplus(decay_row) * rate_gate
    decay_factor = jnp.exp(log_decay) * keep_mask
    scaled = keep_mask * jnp.sqrt(-jnp.expm1(2.0 * log_decay)) + (1.0 - keep_mask)
    return (decay_factor, scaled * input_gate * conv_out)


def contract_last(first_op, second_op):
    return lax.dot_general(
        first_op, second_op, (((1,), (1,)), ((), ())), preferred_element_type=jnp.float32
    )


def contract_first(first_op, second_op):
    return lax.dot_general(
        first_op, second_op, (((0,), (0,)), ((), ())), preferred_element_type=jnp.float32
    )


def blockwise(act_rows, blocks):
    tok_count = act_rows.shape[0]
    block_count, block_size = (blocks.shape[0], blocks.shape[1])
    shaped = act_rows.reshape(tok_count, block_count, block_size)
    return jnp.einsum("tnb,nbc->tnc", shaped, blocks, preferred_element_type=jnp.float32).reshape(
        tok_count, block_count * block_size
    )


def blockwise_back(grad_rows, blocks):
    tok_count = grad_rows.shape[0]
    block_count, block_size = (blocks.shape[0], blocks.shape[1])
    shaped = grad_rows.reshape(tok_count, block_count, block_size)
    return jnp.einsum("tnc,nbc->tnb", shaped, blocks, preferred_element_type=jnp.float32).reshape(
        tok_count, block_count * block_size
    )


def block_outer(act_rows, grad_rows, block_count, block_size):
    tok_count = act_rows.shape[0]
    left_rows = act_rows.reshape(tok_count, block_count, block_size)
    right_rows = grad_rows.reshape(tok_count, block_count, block_size)
    return jnp.einsum("tnb,tnc->nbc", left_rows, right_rows, preferred_element_type=jnp.float32)


def normalize(act_rows, gain_row, full_width):
    squares = lax.psum(jnp.sum(act_rows * act_rows, axis=1), "mp")
    scale_row = lax.rsqrt(squares / full_width + EPS)
    return (act_rows * scale_row[:, None] * gain_row, scale_row)


def unnormalize(act_rows, scale_row, gain_row, grad_normed, full_width):
    inner_sum = lax.psum(jnp.sum(grad_normed * gain_row * act_rows, axis=1), "mp")
    grad_rows = (
        scale_row[:, None] * gain_row * grad_normed
        - act_rows * (scale_row**3 / full_width * inner_sum)[:, None]
    )
    grad_gain = jnp.sum(grad_normed * act_rows * scale_row[:, None], axis=0)
    return (grad_rows, grad_gain)


def widen(act_rows):
    return lax.all_gather(act_rows, "mp", axis=1, tiled=True)


def narrow(partial_rows):
    return lax.psum_scatter(partial_rows, "mp", scatter_dimension=1, tiled=True)


def spread(grad_rows):
    return lax.all_gather(grad_rows, "mp", axis=1, tiled=True)


def collect(partial_rows):
    return lax.psum_scatter(partial_rows, "mp", scatter_dimension=1, tiled=True)


def body(
    inputs,
    cotangent,
    row_split,
    first_gain,
    branch_weight,
    value_weight,
    conv_weight,
    conv_bias,
    rate_blocks,
    input_blocks,
    rate_bias,
    input_bias,
    decay_param,
    out_weight,
    second_gain,
    gate_weight,
    up_weight,
    down_weight,
):
    batches, tok_count, part_width = inputs.shape
    full_width = part_width * lax.axis_size("mp")
    block_count, block_size = (rate_blocks.shape[0], rate_blocks.shape[1])
    lane_count = block_count * block_size
    conv_span = conv_weight.shape[0]
    places = lax.axis_index("dp") * tok_count + lax.iota(jnp.int32, tok_count)
    gain_one = first_gain.astype(jnp.float32)
    gain_two = second_gain.astype(jnp.float32)
    conv_taps = conv_weight.reshape(conv_span, lane_count).astype(jnp.float32)
    conv_shift = conv_bias.reshape(lane_count).astype(jnp.float32)
    rate_shift = rate_bias.reshape(lane_count).astype(jnp.float32)
    input_shift = input_bias.reshape(lane_count).astype(jnp.float32)
    decay_row = decay_param.reshape(lane_count).astype(jnp.float32)
    unit_lanes = jnp.ones((lane_count,), jnp.float32)
    zero_lanes = jnp.zeros((lane_count,), jnp.float32)
    shards = (branch_weight, value_weight, out_weight, gate_weight, up_weight, down_weight)
    outputs = []
    input_grads = []
    totals = None
    for micro_index in range(batches):
        fetched = (
            lax.all_gather(shards[0], "dp", axis=0, tiled=True),
            lax.all_gather(shards[1], "dp", axis=0, tiled=True),
            lax.all_gather(shards[2], "dp", axis=1, tiled=True),
            lax.all_gather(shards[3], "dp", axis=0, tiled=True),
            lax.all_gather(shards[4], "dp", axis=0, tiled=True),
            lax.all_gather(shards[5], "dp", axis=1, tiled=True),
        )
        w_branch, w_value, w_out, w_gate, w_up, w_down = fetched
        act_rows = inputs[micro_index].astype(jnp.float32)
        split_at = row_split[micro_index]
        keep_mask = (places != split_at).astype(jnp.float32)[:, None]
        conv_masks = row_masks(places, split_at, conv_span)
        normed_one, scale_one = normalize(act_rows, gain_one, full_width)
        wide_one = widen(normed_one.astype(jnp.bfloat16))
        branch_pre = jnp.dot(wide_one, w_branch, preferred_element_type=jnp.float32)
        branch = jax.nn.gelu(branch_pre)
        value_pre = jnp.dot(wide_one, w_value, preferred_element_type=jnp.float32)
        border_rows = passed_along(value_pre[tok_count - conv_span + 1 :], "dp", 1)
        extended = jnp.concatenate([border_rows, value_pre], axis=0)
        conv_out = convolve(extended, conv_taps, conv_shift, conv_masks).astype(jnp.bfloat16)
        conv_float = conv_out.astype(jnp.float32)
        rate_pre = blockwise(conv_out, rate_blocks) + rate_shift
        input_pre = blockwise(conv_out, input_blocks) + input_shift
        decay_factor, drive_term = gate_terms(rate_pre, input_pre, conv_float, decay_row, keep_mask)
        decay_prod, local_state = lax.associative_scan(link, (decay_factor, drive_term))
        carry_in = carried_in(
            (decay_prod[-1], local_state[-1]), "dp", link, (unit_lanes, zero_lanes), False
        )
        rnn_state = local_state + decay_prod * carry_in[1]
        mixed_rows = (rnn_state * branch).astype(jnp.bfloat16)
        middle = act_rows + narrow(jnp.dot(mixed_rows, w_out, preferred_element_type=jnp.float32))
        normed_two, scale_two = normalize(middle, gain_two, full_width)
        wide_two = widen(normed_two.astype(jnp.bfloat16))
        gate_pre = jnp.dot(wide_two, w_gate, preferred_element_type=jnp.float32)
        up_pre = jnp.dot(wide_two, w_up, preferred_element_type=jnp.float32)
        hidden = (jax.nn.gelu(gate_pre) * up_pre).astype(jnp.bfloat16)
        result = middle + narrow(jnp.dot(hidden, w_down, preferred_element_type=jnp.float32))
        outputs.append(result.astype(jnp.bfloat16))
        grad_out = cotangent[micro_index]
        wide_cot = spread(grad_out)
        d_hidden = contract_last(wide_cot, w_down)
        g_down = contract_first(hidden, wide_cot)

        def mlp_act(gate_val, up_val):
            return jax.nn.gelu(gate_val) * up_val

        _, pull_mlp = jax.vjp(mlp_act, gate_pre, up_pre)
        d_gate, d_up = pull_mlp(d_hidden)
        d_gate = d_gate.astype(jnp.bfloat16)
        d_up = d_up.astype(jnp.bfloat16)
        back_two = collect(contract_last(d_gate, w_gate) + contract_last(d_up, w_up))
        g_gate = contract_first(wide_two, d_gate)
        g_up = contract_first(wide_two, d_up)
        norm_two, g_gain_two = unnormalize(middle, scale_two, gain_two, back_two, full_width)
        grad_middle = grad_out.astype(jnp.float32) + norm_two
        wide_mid = spread(grad_middle.astype(jnp.bfloat16))
        d_mixed = contract_last(wide_mid, w_out)
        g_out = contract_first(mixed_rows, wide_mid)
        d_state = d_mixed * branch
        _, pull_gelu = jax.vjp(jax.nn.gelu, branch_pre)
        d_branch = pull_gelu(d_mixed * rnn_state)[0].astype(jnp.bfloat16)
        following = jnp.concatenate([decay_factor[1:], unit_lanes[None]], axis=0)
        later_prod, local_adjoint = lax.associative_scan(link, (following, d_state), reverse=True)
        carry_back = carried_in(
            (decay_prod[-1], decay_factor[0] * local_adjoint[0]),
            "dp",
            link,
            (unit_lanes, zero_lanes),
            True,
        )
        adjoint = local_adjoint + later_prod * carry_back[1]
        previous = jnp.concatenate([carry_in[1][None], rnn_state[:-1]], axis=0)

        def gates_only(rate_val, input_val, conv_val, decay_val):
            return gate_terms(rate_val, input_val, conv_val, decay_val, keep_mask)

        _, pull_gates = jax.vjp(gates_only, rate_pre, input_pre, conv_float, decay_row)
        d_rate, d_input, d_conv, d_decay = pull_gates((adjoint * previous, adjoint))
        d_rate = d_rate.astype(jnp.bfloat16)
        d_input = d_input.astype(jnp.bfloat16)
        d_conv = (
            d_conv + blockwise_back(d_rate, rate_blocks) + blockwise_back(d_input, input_blocks)
        )

        def conv_only(ext_val, taps_val, shift_val):
            return convolve(ext_val, taps_val, shift_val, conv_masks)

        _, pull_conv = jax.vjp(conv_only, extended, conv_taps, conv_shift)
        d_extended, g_taps, g_shift = pull_conv(d_conv)
        border_grad = passed_along(d_extended[: conv_span - 1], "dp", -1)
        d_value = d_extended[conv_span - 1 :] + jnp.concatenate(
            [jnp.zeros((tok_count - conv_span + 1, lane_count), jnp.float32), border_grad], axis=0
        )
        d_value = d_value.astype(jnp.bfloat16)
        back_one = collect(contract_last(d_value, w_value) + contract_last(d_branch, w_branch))
        norm_one, g_gain_one = unnormalize(act_rows, scale_one, gain_one, back_one, full_width)
        input_grads.append(grad_middle + norm_one)
        grad_terms = (
            g_gain_one,
            contract_first(wide_one, d_branch),
            contract_first(wide_one, d_value),
            g_taps.reshape(conv_span, block_count, block_size),
            g_shift.reshape(block_count, block_size),
            block_outer(conv_out, d_rate, block_count, block_size),
            block_outer(conv_out, d_input, block_count, block_size),
            jnp.sum(d_rate.astype(jnp.float32), axis=0).reshape(block_count, block_size),
            jnp.sum(d_input.astype(jnp.float32), axis=0).reshape(block_count, block_size),
            d_decay.reshape(block_count, block_size),
            g_out,
            g_gain_two,
            g_gate,
            g_up,
            g_down,
        )
        reduced = (
            lax.psum_scatter(
                grad_terms[0].astype(jnp.bfloat16), "dp", scatter_dimension=0, tiled=True
            ).astype(jnp.float32),
            lax.psum_scatter(
                grad_terms[1].astype(jnp.bfloat16), "dp", scatter_dimension=0, tiled=True
            ).astype(jnp.float32),
            lax.psum_scatter(
                grad_terms[2].astype(jnp.bfloat16), "dp", scatter_dimension=0, tiled=True
            ).astype(jnp.float32),
            lax.psum_scatter(
                grad_terms[3].astype(jnp.bfloat16), "dp", scatter_dimension=2, tiled=True
            ).astype(jnp.float32),
            lax.psum_scatter(
                grad_terms[4].astype(jnp.bfloat16), "dp", scatter_dimension=1, tiled=True
            ).astype(jnp.float32),
            lax.psum_scatter(
                grad_terms[5].astype(jnp.bfloat16), "dp", scatter_dimension=1, tiled=True
            ).astype(jnp.float32),
            lax.psum_scatter(
                grad_terms[6].astype(jnp.bfloat16), "dp", scatter_dimension=1, tiled=True
            ).astype(jnp.float32),
            lax.psum_scatter(
                grad_terms[7].astype(jnp.bfloat16), "dp", scatter_dimension=1, tiled=True
            ).astype(jnp.float32),
            lax.psum_scatter(
                grad_terms[8].astype(jnp.bfloat16), "dp", scatter_dimension=1, tiled=True
            ).astype(jnp.float32),
            lax.psum_scatter(
                grad_terms[9].astype(jnp.bfloat16), "dp", scatter_dimension=1, tiled=True
            ).astype(jnp.float32),
            lax.psum_scatter(
                grad_terms[10].astype(jnp.bfloat16), "dp", scatter_dimension=1, tiled=True
            ).astype(jnp.float32),
            lax.psum_scatter(
                grad_terms[11].astype(jnp.bfloat16), "dp", scatter_dimension=0, tiled=True
            ).astype(jnp.float32),
            lax.psum_scatter(
                grad_terms[12].astype(jnp.bfloat16), "dp", scatter_dimension=0, tiled=True
            ).astype(jnp.float32),
            lax.psum_scatter(
                grad_terms[13].astype(jnp.bfloat16), "dp", scatter_dimension=0, tiled=True
            ).astype(jnp.float32),
            lax.psum_scatter(
                grad_terms[14].astype(jnp.bfloat16), "dp", scatter_dimension=1, tiled=True
            ).astype(jnp.float32),
        )
        if totals is None:
            totals = reduced
        else:
            totals = jax.tree.map(jnp.add, totals, reduced)
    return (jnp.stack(outputs), jnp.stack(input_grads)) + tuple(totals)


def solution(mesh):
    placed = (
        P(None, "dp", "mp"),
        P(None, "dp", "mp"),
        P(),
        P("mp"),
        P("dp", "mp"),
        P("dp", "mp"),
        P(None, "mp", None),
        P("mp", None),
        P("mp", None, None),
        P("mp", None, None),
        P("mp", None),
        P("mp", None),
        P("mp", None),
        P("mp", "dp"),
        P("mp"),
        P("dp", "mp"),
        P("dp", "mp"),
        P("mp", "dp"),
    )
    return jax.shard_map(
        body,
        mesh=mesh,
        in_specs=placed,
        out_specs=(
            P(None, "dp", "mp"),
            P(None, "dp", "mp"),
            P(("mp", "dp")),
            P("dp", "mp"),
            P("dp", "mp"),
            P(None, "mp", "dp"),
            P("mp", "dp"),
            P("mp", "dp", None),
            P("mp", "dp", None),
            P("mp", "dp"),
            P("mp", "dp"),
            P("mp", "dp"),
            P("mp", "dp"),
            P(("mp", "dp")),
            P("dp", "mp"),
            P("dp", "mp"),
            P("mp", "dp"),
        ),
        check_vma=False,
    )
```

profile of v0, /device:TPU:0, one launch (start us, length us, event | category | flops | bytes accessed | tf_op | source)
XLA Modules:
  0.0 2268.1 jit_solution(12225888773444980677)
XLA Ops:
  19.2 16.0 all-reduce.155
  36.2 13.1 all_gather.70
  54.2 13.1 all_gather.80
  314.2 5.3 pad.425
  333.6 5.3 pad.424
  340.1 26.4 %all-gather.2 = f32[16,1,352]{2,1,0:T(1,128)S(1)} all-gather(f32[1,1,352]{2,1,0:T(1,128)S(1)} %reshape.335), channel_id=1, replica_groups=mesh['dp'=16,'mp'=8] {'dp'}, dimensions={0}, use_global_device_ids=true | all-gather | bytes 23936 | tf_op jit(solution)/shard_map/all_gather | solution.py:17
  366.5 5.3 pad.411
  378.6 21.0 all-gather.3
  460.5 22.7 %all-gather.4 = f32[16,1,352]{2,1,0:T(1,128)S(1)} all-gather(f32[1,1,352]{2,1,0:T(1,128)S(1)} %reshape.339), channel_id=1, replica_groups=mesh['dp'=16,'mp'=8] {'dp'}, dimensions={0}, use_global_device_ids=true | all-gather | bytes 23936 | tf_op jit(solution)/shard_map/all_gather | solution.py:17
  491.5 21.0 all-gather.5
  519.2 14.3 all-gather
  533.5 12.6 reduce-scatter.51.cloned.1.call-done
  547.8 13.2 all-reduce.154
  561.6 13.3 all_gather.76
  574.9 20.0 all-gather.21.cloned.1.call-done
  598.1 45.7 %all-gather.23.cloned.1.call-done = bf16[2048,768]{1,0:T(8,128)(2,1)} async-done(((bf16[128,768]{1,0:T(8,128)(2,1)}), bf16[2048,768]{1,0:T(8,128)(2,1)}) %all-gather.23.cloned.1.call-update) | async-done | bytes 3145744 | tf_op jit(solution)/shard_map/all_gather | solution.py:181
  647.1 50.3 %all-gather.25.cloned.1.call-done = bf16[768,2048]{1,0:T(8,128)(2,1)} async-done(((bf16[768,128]{1,0:T(8,128)(2,1)}), bf16[768,2048]{1,0:T(8,128)(2,1)}) %all-gather.25.cloned.1.call-update) | async-done | bytes 3145744 | tf_op jit(solution)/shard_map/all_gather | solution.py:182
  705.8 15.1 all-gather.1
  722.2 15.4 reduce-scatter.55.cloned.1.call-done
  739.6 13.1 all_gather.83
  799.8 12.9 all-reduce.153
  812.7 13.3 reduce-scatter.53.cloned.1.call-done
  827.8 13.1 all_gather.88
  895.5 4.8 slice.1240
  970.6 13.1 all_gather.85
  1066.0 23.3 %all-gather.7 = f32[16,1,352]{2,1,0:T(1,128)S(1)} all-gather(f32[1,1,352]{2,1,0:T(1,128)S(1)} %reshape.345), channel_id=1, replica_groups=mesh['dp'=16,'mp'=8] {'dp'}, dimensions={0}, use_global_device_ids=true | all-gather | bytes 23936 | tf_op jit(solution)/shard_map/all_gather | solution.py:17
  1089.4 11.6 while.59
  1108.2 22.5 all-gather.6
  1131.0 11.6 while.58
  1166.7 5.7 collective-permute-done.2
  1178.2 4.8 collective-permute-done.3
  1222.4 11.6 all-reduce.160.cloned.1.call-done
  1235.4 77.1 %reduce-scatter.83.cloned.1.call-done = bf16[128,768]{1,0:T(8,128)(2,1)} async-done(((bf16[2048,768]{1,0:T(8,128)(2,1)}), bf16[128,768]{1,0:T(8,128)(2,1)}) %reduce-scatter.83.cloned.1.call-update) | async-done | bytes 196624
  1313.6 32.6 %reduce-scatter.57.cloned.1.call-done = f32[128,256]{1,0:T(8,128)} async-done(((f32[128,2048]{1,0:T(8,128)}), f32[128,256]{1,0:T(8,128)}) %reduce-scatter.57.cloned.1.call-update) | async-done | bytes 131088 | tf_op jit(solution)/shard_map/reduce_scatter | solution.py:133
  1346.1 33.0 %reduce-scatter.61.cloned.1.call-done = f32[128,256]{1,0:T(8,128)} async-done(((f32[128,2048]{1,0:T(8,128)}), f32[128,256]{1,0:T(8,128)}) %reduce-scatter.61.cloned.1.call-update) | async-done | bytes 131088 | tf_op jit(solution)/shard_map/reduce_scatter | solution.py:133
  1380.4 74.3 %all-reduce.156 = (bf16[256]{0:T(256)(128)(2,1)S(1)}, bf16[256]{0:T(256)(128)(2,1)S(1)}, bf16[4,2,176]{2,1,0:T(2,128)(2,1)S(1)}, bf16[4,2,176]{2,1,0:T(2,128)(2,...) all-reduce(bf16[256]{0:T(256)(128)(2,1)S(1)} %get-tuple-element.521, ...), channel_id=13, replica_groups=mesh['dp'=16,'mp'=8] {'dp'}, use_global_device_ids=true, to_apply=%region_35.37.clone | all-reduce | flops 6656 | bytes 26624
  1454.6 12.7 all-reduce.152
  1473.6 14.0 reduce-scatter.81.cloned.1.call-done
  1488.6 75.0 %reduce-scatter.79.cloned.1.call-done = bf16[128,352]{1,0:T(8,128)(2,1)} async-done(((bf16[2048,352]{1,0:T(8,128)(2,1)}), bf16[128,352]{1,0:T(8,128)(2,1)}) %reduce-scatter.79.cloned.1.call-update) | async-done | bytes 90128
  1564.6 75.1 %reduce-scatter.73.cloned.1.call-done = bf16[128,352]{1,0:T(8,128)(2,1)} async-done(((bf16[2048,352]{1,0:T(8,128)(2,1)}), bf16[128,352]{1,0:T(8,128)(2,1)}) %reduce-scatter.73.cloned.1.call-update) | async-done | bytes 90128
  1640.8 74.9 %reduce-scatter.71.cloned.1.call-done = bf16[128,352]{1,0:T(8,128)(2,1)} async-done(((bf16[2048,352]{1,0:T(8,128)(2,1)}), bf16[128,352]{1,0:T(8,128)(2,1)}) %reduce-scatter.71.cloned.1.call-update) | async-done | bytes 90128
  1718.1 73.7 %reduce-scatter.77.cloned.1.call-done = bf16[128,352]{1,0:T(8,128)(2,1)} async-done(((bf16[2048,352]{1,0:T(8,128)(2,1)}), bf16[128,352]{1,0:T(8,128)(2,1)}) %reduce-scatter.77.cloned.1.call-update) | async-done | bytes 90128
  1792.8 75.1 %reduce-scatter.75.cloned.1.call-done = bf16[128,352]{1,0:T(8,128)(2,1)} async-done(((bf16[2048,352]{1,0:T(8,128)(2,1)}), bf16[128,352]{1,0:T(8,128)(2,1)}) %reduce-scatter.75.cloned.1.call-update) | async-done | bytes 90128
  1869.7 76.6 %reduce-scatter.85.cloned.1.call-done = bf16[128,768]{1,0:T(8,128)(2,1)} async-done(((bf16[2048,768]{1,0:T(8,128)(2,1)}), bf16[128,768]{1,0:T(8,128)(2,1)}) %reduce-scatter.85.cloned.1.call-update) | async-done | bytes 196624
  1948.2 76.4 %reduce-scatter.63.cloned.1.call-done = bf16[128,768]{1,0:T(8,128)(2,1)} async-done(((bf16[2048,768]{1,0:T(8,128)(2,1)}), bf16[128,768]{1,0:T(8,128)(2,1)}) %reduce-scatter.63.cloned.1.call-update) | async-done | bytes 196624 | tf_op jit(solution)/shard_map/reduce_scatter | solution.py:328
  2024.6 78.2 %reduce-scatter.65.cloned.1.call-done = bf16[128,768]{1,0:T(8,128)(2,1)} async-done(((bf16[2048,768]{1,0:T(8,128)(2,1)}), bf16[128,768]{1,0:T(8,128)(2,1)}) %reduce-scatter.65.cloned.1.call-update) | async-done | bytes 196624 | tf_op jit(solution)/shard_map/reduce_scatter | solution.py:328
  2104.6 76.3 %reduce-scatter.67.cloned.1.call-done = bf16[128,768]{1,0:T(8,128)(2,1)} async-done(((bf16[2048,768]{1,0:T(8,128)(2,1)}), bf16[128,768]{1,0:T(8,128)(2,1)}) %reduce-scatter.67.cloned.1.call-update) | async-done | bytes 196624 | tf_op jit(solution)/shard_map/reduce_scatter | solution.py:331
  2180.9 78.1 %reduce-scatter.69.cloned.1.call-done = bf16[128,768]{1,0:T(8,128)(2,1)} async-done(((bf16[2048,768]{1,0:T(8,128)(2,1)}), bf16[128,768]{1,0:T(8,128)(2,1)}) %reduce-scatter.69.cloned.1.call-update) | async-done | bytes 196624 | tf_op jit(solution)/shard_map/reduce_scatter | solution.py:331
  (1273 shorter events, 756.9 us)
Async XLA Ops:
  7.2 60.1 %all-gather.15.cloned.1.call-start = ((), (), s32[]{:S(2)}) async-start(), calls=%async_computation.20 | async-start | bytes 1531904 | tf_op jit(solution)/shard_map/all_gather | solution.py:178
  7.9 392.8 %all-gather.17.cloned.1.call-start = ((), (), s32[]{:S(2)}) async-start(), calls=%async_computation.21 | async-start | bytes 1531904 | tf_op jit(solution)/shard_map/all_gather | solution.py:177
  8.7 394.8 %all-gather.19.cloned.1.call-start = ((), (), s32[]{:S(2)}) async-start(), calls=%async_computation.22 | async-start | bytes 1531904 | tf_op jit(solution)/shard_map/all_gather | solution.py:179
  9.4 524.1 %reduce-scatter.47.cloned.1.call-start = ((), (), s32[]{:S(2)}) async-start(), calls=%async_computation.23 | async-start | bytes 1179648 | tf_op jit(solution)/shard_map/reduce_scatter | solution.py:125
  49.3 351.4 %copy-start.7 = (bf16[128,2048]{1,0:T(8,128)(2,1)}, bf16[128,2048]{1,0:T(8,128)(2,1)S(1)}, u32[]{:S(2)}) copy-start(bf16[128,2048]{1,0:T(8,128)(2,1)S(1)} %all_gather.70) | copy-start | bytes 1572868
  67.3 446.3 %copy-start.9 = (bf16[128,2048]{1,0:T(8,128)(2,1)}, bf16[128,2048]{1,0:T(8,128)(2,1)S(1)}, u32[]{:S(2)}) copy-start(bf16[128,2048]{1,0:T(8,128)(2,1)S(1)} %all_gather.80) | copy-start | bytes 1572868
  69.5 8.9 collective-permute-start
  75.0 7.4 collective-permute-start.1
  90.8 365.4 %copy-start.17 = (f32[128,352]{0,1:T(8,128)}, f32[128,352]{0,1:T(8,128)S(1)}, u32[]{:S(2)}) copy-start(f32[128,352]{0,1:T(8,128)S(1)} %get-tuple-element.801) | copy-start | bytes 540676
  406.4 139.7 %reduce-scatter.51.cloned.1.call-start = ((), (), s32[]{:S(2)}) async-start(), calls=%async_computation.28 | async-start | bytes 1179648 | tf_op jit(solution)/shard_map/reduce_scatter | solution.py:125
  516.4 78.5 %all-gather.21.cloned.1.call-start = ((), (), s32[]{:S(2)}) async-start(), calls=%async_computation.24 | async-start | bytes 3342336 | tf_op jit(solution)/shard_map/all_gather | solution.py:180
  517.0 126.9 %all-gather.23.cloned.1.call-start = ((), (), s32[]{:S(2)}) async-start(), calls=%async_computation.25 | async-start | bytes 3342336 | tf_op jit(solution)/shard_map/all_gather | solution.py:181
  517.7 179.7 %all-gather.25.cloned.1.call-start = ((), (), s32[]{:S(2)}) async-start(), calls=%async_computation.26 | async-start | bytes 3342336 | tf_op jit(solution)/shard_map/all_gather | solution.py:182
  518.5 219.2 %reduce-scatter.55.cloned.1.call-start = ((), (), s32[]{:S(2)}) async-start(), calls=%async_computation.30 | async-start | bytes 1179648 | tf_op jit(solution)/shard_map/reduce_scatter | solution.py:133
  705.8 92.4 %reduce-scatter.59.cloned.1.call-start = ((), (), s32[]{:S(2)}) async-start(), calls=%async_computation.32 | async-start | bytes 1179648 | tf_op jit(solution)/shard_map/reduce_scatter | solution.py:133
  760.9 65.2 %reduce-scatter.53.cloned.1.call-start = ((), (), s32[]{:S(2)}) async-start(), calls=%async_computation.29 | async-start | bytes 1179648 | tf_op jit(solution)/shard_map/reduce_scatter | solution.py:125
  763.4 470.6 %all-reduce.160.cloned.1.call-start = ((), (), s32[]{:S(2)}) async-start(), calls=%async_computation.46 | async-start | bytes 1441792
  1151.2 161.2 %reduce-scatter.83.cloned.1.call-start = ((), (), s32[]{:S(2)}) async-start(), calls=%async_computation.44 | async-start | bytes 3342336
  1156.6 189.5 %reduce-scatter.57.cloned.1.call-start = ((), (), s32[]{:S(2)}) async-start(), calls=%async_computation.31 | async-start | bytes 1179648 | tf_op jit(solution)/shard_map/reduce_scatter | solution.py:133
  1164.9 7.5 collective-permute-start.2
  1174.1 205.1 %reduce-scatter.61.cloned.1.call-start = ((), (), s32[]{:S(2)}) async-start(), calls=%async_computation.33 | async-start | bytes 1179648 | tf_op jit(solution)/shard_map/reduce_scatter | solution.py:133
  1175.5 7.5 collective-permute-start.3
  1184.7 285.3 %reduce-scatter.49.cloned.1.call-start = ((), (), s32[]{:S(2)}) async-start(), calls=%async_computation.27 | async-start | bytes 1179648 | tf_op jit(solution)/shard_map/reduce_scatter | solution.py:125
  1188.3 299.3 %reduce-scatter.81.cloned.1.call-start = ((), (), s32[]{:S(2)}) async-start(), calls=%async_computation.43 | async-start | bytes 1671168
  1190.5 373.1 %reduce-scatter.79.cloned.1.call-start = ((), (), s32[]{:S(2)}) async-start(), calls=%async_computation.42 | async-start | bytes 1671168
  1192.8 447.0 %reduce-scatter.73.cloned.1.call-start = ((), (), s32[]{:S(2)}) async-start(), calls=%async_computation.39 | async-start | bytes 1671168
  1195.0 520.7 %reduce-scatter.71.cloned.1.call-start = ((), (), s32[]{:S(2)}) async-start(), calls=%async_computation.38 | async-start | bytes 1671168
  1197.5 594.3 %reduce-scatter.77.cloned.1.call-start = ((), (), s32[]{:S(2)}) async-start(), calls=%async_computation.41 | async-start | bytes 1671168
  1199.7 668.2 %reduce-scatter.75.cloned.1.call-start = ((), (), s32[]{:S(2)}) async-start(), calls=%async_computation.40 | async-start | bytes 1671168
  1201.9 744.4 %reduce-scatter.85.cloned.1.call-start = ((), (), s32[]{:S(2)}) async-start(), calls=%async_computation.45 | async-start | bytes 3342336
  1206.9 817.7 %reduce-scatter.63.cloned.1.call-start = ((), (), s32[]{:S(2)}) async-start(), calls=%async_computation.34 | async-start | bytes 3342336 | tf_op jit(solution)/shard_map/reduce_scatter | solution.py:328
  1210.6 892.2 %reduce-scatter.65.cloned.1.call-start = ((), (), s32[]{:S(2)}) async-start(), calls=%async_computation.35 | async-start | bytes 3342336 | tf_op jit(solution)/shard_map/reduce_scatter | solution.py:328
  1213.4 967.6 %reduce-scatter.67.cloned.1.call-start = ((), (), s32[]{:S(2)}) async-start(), calls=%async_computation.36 | async-start | bytes 3342336 | tf_op jit(solution)/shard_map/reduce_scatter | solution.py:331
  1216.3 1042.7 %reduce-scatter.69.cloned.1.call-start = ((), (), s32[]{:S(2)}) async-start(), calls=%async_computation.37 | async-start | bytes 3342336 | tf_op jit(solution)/shard_map/reduce_scatter | solution.py:331
  1219.0 161.3 %copy-start.198 = (bf16[256]{0:T(256)(128)(2,1)S(1)}, bf16[256]{0:T(256)(128)(2,1)}, u32[]{:S(2)}) copy-start(bf16[256]{0:T(256)(128)(2,1)} %get-tuple-element.515) | copy-start | bytes 1540
  1219.0 161.3 %copy-start.199 = (bf16[256]{0:T(256)(128)(2,1)S(1)}, bf16[256]{0:T(256)(128)(2,1)}, u32[]{:S(2)}) copy-start(bf16[256]{0:T(256)(128)(2,1)} %get-tuple-element.517) | copy-start | bytes 1540
  1219.0 250.9 %copy-start.204 = (f32[128]{0:T(128)S(1)}, f32[128]{0:T(128)}, u32[]{:S(2)}) copy-start(f32[128]{0:T(128)} %copy-done.203) | copy-start | bytes 1540
  1219.1 250.9 %copy-start.206 = (f32[128]{0:T(128)S(1)}, f32[128]{0:T(128)}, u32[]{:S(2)}) copy-start(f32[128]{0:T(128)} %copy-done.205) | copy-start | bytes 1540
  1219.1 250.9 %copy-start.50 = (f32[128,256]{1,0:T(8,128)S(1)}, f32[128,256]{1,0:T(8,128)}, u32[]{:S(2)}) copy-start(f32[128,256]{1,0:T(8,128)} %copy-done.48) | copy-start | bytes 393220
  1219.1 250.9 %copy-start.77 = (f32[128,256]{1,0:T(8,128)S(1)}, f32[128,256]{1,0:T(8,128)}, u32[]{:S(2)}) copy-start(f32[128,256]{1,0:T(8,128)} %reduce-scatter.55.cloned.1.call-done) | copy-start | bytes 393220
  1219.1 250.9 %copy-start.80 = (bf16[2,128,256]{2,1,0:T(8,128)(2,1)S(1)}, bf16[2,128,256]{2,1,0:T(8,128)(2,1)}, u32[]{:S(2)}) copy-start(bf16[2,128,256]{2,1,0:T(8,128)(2,1)} %param.28) | copy-start | bytes 393220
  1219.1 250.9 %copy-start.162 = (f32[128]{0:T(128)S(1)}, f32[128]{0:T(128)}, u32[]{:S(2)}) copy-start(f32[128]{0:T(128)} %copy-done.160) | copy-start | bytes 1540
  1219.1 250.9 %copy-start.201 = (f32[128]{0:T(128)S(1)}, f32[128]{0:T(128)}, u32[]{:S(2)}) copy-start(f32[128]{0:T(128)} %copy-done.200) | copy-start | bytes 1540
  1219.1 252.0 %copy-start.132 = (bf16[1,128,256]{2,1,0:T(8,128)(2,1)S(1)}, bf16[1,128,256]{2,1,0:T(8,128)(2,1)}, u32[]{:S(2)}) copy-start(bf16[1,128,256]{2,1,0:T(8,128)(2,1)} %get-tuple-element.779) | copy-start | bytes 196612
  1219.1 252.7 %copy-start.45 = (f32[128,256]{1,0:T(8,128)S(1)}, f32[128,256]{1,0:T(8,128)}, u32[]{:S(2)}) copy-start(f32[128,256]{1,0:T(8,128)} %get-tuple-element.785) | copy-start | bytes 393220
  1219.1 252.7 %copy-start.75 = (f32[128,256]{1,0:T(8,128)S(1)}, f32[128,256]{1,0:T(8,128)}, u32[]{:S(2)}) copy-start(f32[128,256]{1,0:T(8,128)} %reduce-scatter.59.cloned.1.call-done) | copy-start | bytes 393220
  1219.2 252.7 %copy-start.149 = (f32[128]{0:T(128)S(1)}, f32[128]{0:T(128)}, u32[]{:S(2)}) copy-start(f32[128]{0:T(128)} %add_rsqrt_fusion) | copy-start | bytes 1540
  1219.2 252.7 %copy-start.197 = (f32[128]{0:T(128)S(1)}, f32[128]{0:T(128)}, u32[]{:S(2)}) copy-start(f32[128]{0:T(128)} %copy-done.196) | copy-start | bytes 1540
  (195 other events, 4862.9 us)
Sparse Core Ops, SparseCore 0:
  10.2 47.1 all-gather.14
  59.5 44.9 all-gather.16
  106.6 44.1 all-gather.18
  406.6 29.5 reduce-scatter.46
  516.5 29.5 reduce-scatter.50
  548.1 46.7 all-gather.20
  597.1 46.7 all-gather.22
  646.0 51.3 all-gather.24
  705.9 31.6 reduce-scatter.54
  761.0 31.7 reduce-scatter.58
  795.1 30.8 reduce-scatter.52
  1151.4 82.5 all-reduce.159
  1237.3 75.0 reduce-scatter.82
  1314.7 31.3 reduce-scatter.56
  1348.4 30.7 reduce-scatter.60
  1381.4 30.7 reduce-scatter.48
  1415.3 72.2 reduce-scatter.80
  1490.7 72.8 reduce-scatter.78
  1566.9 72.8 reduce-scatter.72
  1642.8 72.8 reduce-scatter.70
  1718.9 72.8 reduce-scatter.76
  1795.0 72.8 reduce-scatter.74
  1871.3 74.9 reduce-scatter.84
  1949.5 75.0 reduce-scatter.62
  2027.9 74.8 reduce-scatter.64
  2106.0 74.8 reduce-scatter.66
  2184.1 74.8 reduce-scatter.68
where the time goes:
time: 2280 us; the launch traced here: 2270 us
  waiting for transfers between devices  1100 us (48%)
  local copies, waits for them, and re-layouts  519 us (23%)
  blocking collectives  374 us (16%)
  other arithmetic  168 us (7%)
  matrix products  68.8 us (3%)
    unnamed x36, waiting for transfers between devices  558 us
    reduce_scatter x2, waiting for transfers between devices, body(): lax.psum_scatter(grad_terms[12].astype(jnp.bfloat16), 'dp', scatter_dimen...  155 us
    reduce_scatter x2, waiting for transfers between devices, body(): lax.psum_scatter(grad_terms[13].astype(jnp.bfloat16), 'dp', scatter_dimen...  154 us
    all_gather x6, blocking collectives, carried_in(): pieces = jax.tree.map(lambda part: lax.all_gather(part, axis), value)  137 us
    slice x84, local copies, waits for them, and re-layouts, body(): lax.associative_scan(link, (following, d_state), reverse=True)  121 us
    slice x70, local copies, waits for them, and re-layouts, body(): lax.associative_scan(link, (decay_factor, drive_term))  117 us
    pad x48, local copies, waits for them, and re-layouts, body(): lax.associative_scan(link, (decay_factor, drive_term))  115 us
    reduce_scatter x4, waiting for transfers between devices, collect(): return lax.psum_scatter(partial_rows, 'mp', scatter_dimension=1, tiled=True)  81 us
  transfers between devices with their start and end apart: 31, of which 24 were waited for; matrix products, arithmetic and copies ran while one was open for 21% of the time, Pallas kernels for 0%

commit v1 on v0

v1 whole, which is shorter than its diff:
```python
import functools
import math

import jax
import jax.numpy as jnp
from jax import lax
from jax.experimental import pallas as pl
from jax.experimental.pallas import tpu as pltpu
from jax.sharding import PartitionSpec as P

EPS = 1e-06
F32 = jnp.float32
BF16 = jnp.bfloat16
NT = (((1,), (1,)), ((), ()))
TN = (((0,), (0,)), ((), ()))
HALO = 16
SIDE = 4
VMEM_BYTES = 56 * 1024 * 1024
FLOPS_PER_US = 1.15e9
COST_US = {
    "norm_one": 3.5, "rec_fwd": 8.4, "rec_out": 3.7, "ffn": 12.9, "ffn_grad_one": 5.0, "ffn_grad_two": 0.3,
    "ffn_grad_three": 6.3, "ffn_out": 15.0, "dn2_sum": 0.3, "rec_bwd": 0.3, "early_grad": 0.3,
    "early_out": 1.7,
    "gate_bwd": 3.9, "conv_bwd": 5.7, "late_grad": 0.3, "finish": 2.8, "small_out": 1.5, "late_out": 2.5,
}
GELU_K = math.sqrt(2.0 / math.pi)


def mm(a, b):
    return jnp.dot(a, b, preferred_element_type=F32)


def mm_nt(a, b):
    return lax.dot_general(a, b, NT, preferred_element_type=F32)


def mm_tn(a, b):
    return lax.dot_general(a, b, TN, preferred_element_type=F32)


def gelu_pair(x):
    t = jnp.tanh(GELU_K * (x + 0.044715 * (x * x * x)))
    half = 0.5 * (1.0 + t)
    slope = half + 0.5 * x * (1.0 - t * t) * (GELU_K * (1.0 + 0.134145 * (x * x)))
    return x * half, slope


def neg_expm1(x):
    near = jnp.maximum(x, -0.5)
    series = 1.0 / 40320.0 + near * (1.0 / 362880.0)
    for denom in (5040.0, 720.0, 120.0, 24.0, 6.0, 2.0, 1.0):
        series = 1.0 / denom + near * series
    return jnp.where(x > -0.5, -near * series, 1.0 - jnp.exp(x))


def rolled(x, by):
    return x if by == 0 else jnp.roll(x, by, axis=0)


def shift_down(x, step, fill):
    rows = lax.broadcasted_iota(jnp.int32, x.shape, 0)
    return jnp.where(rows < step, fill, jnp.roll(x, step, axis=0))


def shift_up(x, step, fill):
    count = x.shape[0]
    rows = lax.broadcasted_iota(jnp.int32, x.shape, 0)
    return jnp.where(rows >= count - step, fill, jnp.roll(x, -step, axis=0))


def scan_down(a, u):
    step = 1
    while step < a.shape[0]:
        u = u + a * shift_down(u, step, 0.0)
        a = a * shift_down(a, step, 1.0)
        step *= 2
    return a, u


def scan_up(a, u):
    step = 1
    while step < a.shape[0]:
        u = u + a * shift_up(u, step, 0.0)
        a = a * shift_up(a, step, 1.0)
        step *= 2
    return a, u


def conv_mask(place, split_at, back):
    behind = place - back
    return ((behind >= split_at) == (place >= split_at)) & (behind >= 0)


def call(kernel, outs, ins, args, grid=None, out_specs=None, scratch=(), name=None, ties=()):
    kwargs = {}
    if ties:
        count, inner = len(args), kernel

        def kernel(*refs):
            inner(*refs[:count], *refs[count + len(ties) :])

        ins = list(ins) + [pl.BlockSpec(memory_space=pl.ANY)] * len(ties)
        args = tuple(args) + tuple(ties)
    if grid is not None:
        kwargs["grid"] = grid
    return pl.pallas_call(
        kernel,
        out_shape=outs,
        in_specs=ins,
        out_specs=out_specs if out_specs is not None else [WHOLE] * len(outs),
        scratch_shapes=list(scratch),
        compiler_params=pltpu.CompilerParams(vmem_limit_bytes=VMEM_BYTES),
        cost_estimate=pl.CostEstimate(flops=int(COST_US[name] * FLOPS_PER_US), bytes_accessed=0, transcendentals=0),
        name=name,
        **kwargs,
    )(*args)


WHOLE = pl.BlockSpec(memory_space=pltpu.VMEM)
SCALARS = pl.BlockSpec(memory_space=pltpu.SMEM)
ME, ROW_Y, COL_X, DEEP_Z, CORE = 2, 3, 4, 5, 6
NEAR = (0, -1, 1)


def shape(dims, dtype=F32):
    return jax.ShapeDtypeStruct(dims, dtype)


def lane_block(index, width):
    return pl.ds(pl.multiple_of(index * width, width), width)


def lay_parts(s_ref, three, far, three_other, far_other, put):
    z, core = s_ref[DEEP_Z], s_ref[CORE]
    for held, held_far, which in ((three, far, core), (three_other, far_other, 1 - core)):
        for k, dz in enumerate(NEAR):
            put((z + dz + SIDE) % SIDE * 2 + which, held[k])
        put((z + 2) % SIDE * 2 + which, held_far[...])


def norm_one_kernel(s_ref, three, far, three_other, far_other, n1_ref, own_ref, rho_ref, gain_ref, x_ref):
    rows = three.shape[1] - HALO
    width = three.shape[2]
    full = x_ref.shape[1]

    def put(block, value):
        here = lane_block(block, width)
        x_ref[:, here] = value[:rows]
        gain_ref[:, here] = value[rows:].astype(F32)

    lay_parts(s_ref, three, far, three_other, far_other, put)
    total = jnp.zeros((rows, 1), F32)
    for j in range(full // width):
        xj = x_ref[:, j * width : (j + 1) * width].astype(F32)
        total = total + jnp.sum(xj * xj, axis=1, keepdims=True)
    rho = lax.rsqrt(total / full + EPS)
    rho_ref[...] = rho
    batches = own_ref.shape[0] // (rows // 2 - HALO)
    ext = rows // batches
    toks = ext - HALO
    for j in range(full // width):
        here = slice(j * width, (j + 1) * width)
        n1 = (x_ref[:, here].astype(F32) * rho * gain_ref[0:1, here]).astype(BF16)
        n1_ref[:, here] = n1
        for m in range(batches):
            own_ref[m * toks : (m + 1) * toks, here] = n1[m * ext + HALO : (m + 1) * ext]


def rec_fwd_kernel(s_ref, n1_ref, shards_ref, vec_ref, wr_ref, wi_ref,
                   w_ref, yb_ref, vb_ref, c_ref, r_ref, i_ref, a_ref, pr_ref, st_ref, last_ref):
    batches = 2
    ext = n1_ref.shape[0] // batches
    toks = ext - HALO
    lanes = vec_ref.shape[1]
    piece = shards_ref.shape[2]
    for i in range(shards_ref.shape[0]):
        w_ref[:, i * piece : (i + 1) * piece] = shards_ref[i]
    start = s_ref[ME] * toks
    vb_ref[...] = mm_nt(n1_ref[...], w_ref[lanes : 2 * lanes])
    last_ref[...] = jnp.zeros_like(last_ref)
    for m in range(batches):
        own = slice(m * toks, (m + 1) * toks)
        yb_ref[own] = mm_nt(n1_ref[m * ext + HALO : (m + 1) * ext], w_ref[:lanes])
        vb = vb_ref[m * ext : (m + 1) * ext]
        place = start + lax.broadcasted_iota(jnp.int32, (toks, lanes), 0)
        split_at = s_ref[m]
        conv = jnp.zeros((toks, lanes), F32) + vec_ref[4:5]
        for k in range(4):
            term = vec_ref[k : k + 1] * rolled(vb, k)[HALO:]
            conv = conv + jnp.where(conv_mask(place, split_at, k), term, 0.0)
        c16 = conv.astype(BF16)
        c = c16.astype(F32)
        rate = jax.nn.sigmoid(mm(c16, wr_ref[...]) + vec_ref[5:6])
        gate = jax.nn.sigmoid(mm(c16, wi_ref[...]) + vec_ref[6:7])
        la = -vec_ref[7:8] * rate
        keep = (place != split_at).astype(F32)
        a = keep * jnp.exp(la)
        u = (keep * jnp.sqrt(neg_expm1(2.0 * la)) + (1.0 - keep)) * gate * c
        c_ref[own] = c16
        r_ref[own] = rate
        i_ref[own] = gate
        a_ref[own] = a
        prod, state = scan_down(a, u)
        pr_ref[own] = prod
        st_ref[own] = state
        last_ref[2 * m : 2 * m + 1] = prod[toks - 1 :]
        last_ref[2 * m + 1 : 2 * m + 2] = state[toks - 1 :]


def carry_of(s_ref, all_ref, m, backward):
    me = s_ref[ME]
    count = all_ref.shape[0]
    carry = jnp.zeros((1, all_ref.shape[2]), F32)
    for q in range(count - 1, 0, -1) if backward else range(count - 1):
        longer = all_ref[q, 2 * m : 2 * m + 1] * carry + all_ref[q, 2 * m + 1 : 2 * m + 2]
        carry = jnp.where((q > me) if backward else (q < me), longer, carry)
    return carry


def chunk_places(s_ref):
    z, core = s_ref[DEEP_Z], s_ref[CORE]
    for r in range(SIDE):
        yield r, (z + r) % SIDE * 2 + core, (z + r) % SIDE * 2 + 1 - core


def rec_out_kernel(s_ref, all_ref, pr_ref, st_ref, yb_ref, w_ref,
                   h_ref, carry_ref, o_ref, keep_ref, swap_ref):
    batches = 2
    toks = pr_ref.shape[0] // batches
    carry_ref[...] = jnp.zeros_like(carry_ref)
    for m in range(batches):
        own = slice(m * toks, (m + 1) * toks)
        carry = carry_of(s_ref, all_ref, m, False)
        carry_ref[m : m + 1] = carry
        h = st_ref[own] + pr_ref[own] * carry
        h_ref[own] = h
        o_ref[own] = (h * gelu_pair(yb_ref[own])[0]).astype(BF16)
    width = keep_ref.shape[2]
    for r, mine, other in chunk_places(s_ref):
        swap_ref[r] = mm(o_ref[...], w_ref[:, lane_block(other, width)]).astype(BF16)
        keep_ref[r] = mm(o_ref[...], w_ref[:, lane_block(mine, width)]).astype(BF16)


def inner_rows(products):
    ones = jnp.ones((HALO, products.shape[1]), F32)
    sums = lax.dot_general(ones, products, NT, precision=lax.Precision.HIGHEST, preferred_element_type=F32)
    high = sums.astype(BF16)
    low = (sums - high.astype(F32)).astype(BF16)
    rows = lax.broadcasted_iota(jnp.int32, sums.shape, 0)
    return jnp.where(rows == 0, high.astype(F32), jnp.where(rows == 1, low.astype(F32), 0.0)).astype(BF16)


def ffn_kernel(s_ref, three, far, three_other, far_other, c3_ref, cf_ref, c3o_ref, cfo_ref, gain_ref, w_ref,
               n2_ref, x2_ref, rho_ref, cotf_ref, hid_ref, dgt_ref, dup_ref, po_ref, keep_ref, swap_ref,
               acc_o, acc_d, acc_i):
    step = pl.program_id(0)
    deep, _, rows, cols = w_ref.shape
    _, toks, width = three.shape
    parts = x2_ref.shape[1] // width

    @pl.when(step == 0)
    def _():
        def put(block, value):
            x2_ref[:, lane_block(block, width)] = value

        def put_cot(block, value):
            cotf_ref[:, lane_block(block, width)] = value

        lay_parts(s_ref, three, far, three_other, far_other, put)
        lay_parts(s_ref, c3_ref, cf_ref, c3o_ref, cfo_ref, put_cot)
        total = jnp.zeros((toks, 1), F32)
        for j in range(parts):
            here = slice(j * width, (j + 1) * width)
            xj = x2_ref[:, here].astype(F32)
            total = total + jnp.sum(xj * xj, axis=1, keepdims=True)
        rho = lax.rsqrt(total / (parts * width) + EPS)
        rho_ref[...] = rho
        for j in range(parts):
            here = slice(j * width, (j + 1) * width)
            n2_ref[:, here] = (x2_ref[:, here].astype(F32) * rho * gain_ref[1:2, here]).astype(BF16)
        acc_o[...] = jnp.zeros_like(acc_o)
        acc_d[...] = jnp.zeros_like(acc_d)
        acc_i[...] = jnp.zeros_like(acc_i)

    wg = w_ref[:, 0].reshape(deep * rows, cols)
    wu = w_ref[:, 1].reshape(deep * rows, cols)
    wd = w_ref[:, 2].reshape(deep * rows, cols)
    gt = mm(n2_ref[...], wg)
    up = mm(n2_ref[...], wu)
    dm = mm(cotf_ref[...], wd)
    act, slope = gelu_pair(gt)
    hid = (act * up).astype(BF16)
    dgt = (slope * up * dm).astype(BF16)
    dup = (act * dm).astype(BF16)
    hid_ref[...] = hid
    dgt_ref[...] = dgt
    dup_ref[...] = dup
    acc_i[...] += dgt.astype(F32) * gt + dup.astype(F32) * up
    acc_o[...] += mm_nt(hid, wd)
    acc_d[...] += mm_nt(dgt, wg) + mm_nt(dup, wu)

    @pl.when(step == pl.num_programs(0) - 1)
    def _():
        side = inner_rows(acc_i[...])
        po_ref[...] = acc_o[...].astype(BF16)
        core = s_ref[CORE]
        for z in range(SIDE):
            for ref, block in ((swap_ref, 2 * z + 1 - core), (keep_ref, 2 * z + core)):
                ref[z, :toks] = acc_d[:, lane_block(block, width)].astype(BF16)
                ref[z, toks:] = side


def rec_bwd_kernel(s_ref, dn2_ref, other_ref, x2_ref, cotf_ref, gain_ref, rho_ref, inner_ref, w_ref,
                   yb_ref, h_ref, a_ref, pr_ref,
                   gr_ref, dyb_ref, la_ref, lp_ref, first_ref):
    width = dn2_ref.shape[2]
    full = x2_ref.shape[1]
    batches = 2
    toks = x2_ref.shape[0] // batches
    rho = rho_ref[...]
    back = rho * rho * rho / full * inner_ref[...]

    core = s_ref[CORE]
    for z in range(SIDE):
        for ref, block in ((dn2_ref, 2 * z + core), (other_ref, 2 * z + 1 - core)):
            here = lane_block(block, width)
            gx2 = (cotf_ref[:, here].astype(F32) + rho * gain_ref[1:2, here] * ref[z].astype(F32)
                   - x2_ref[:, here].astype(F32) * back)
            gr_ref[:, here] = gx2.astype(BF16)
    do = mm_nt(gr_ref[...], w_ref[...])
    ends = []
    for m in range(batches):
        own = slice(m * toks, (m + 1) * toks)
        act, slope = gelu_pair(yb_ref[own])
        dom = do[own]
        dyb_ref[own] = (slope * h_ref[own] * dom).astype(BF16)
        a = a_ref[own]
        prod, adj = scan_up(shift_up(a, 1, 1.0), dom * act)
        la_ref[own] = adj
        lp_ref[own] = prod
        ends += [pr_ref[(m + 1) * toks - 1 : (m + 1) * toks], a[0:1] * adj[0:1]]
    ends = jnp.concatenate(ends + [jnp.zeros_like(ends[0])] * (first_ref.shape[1] - len(ends)), axis=0)
    for i in range(first_ref.shape[0]):
        first_ref[i] = ends


def gate_bwd_kernel(s_ref, all_ref, la_ref, lp_ref, a_ref, h_ref, carry_ref, c_ref, r_ref,
                    i_ref, vec_ref, wr_ref, wi_ref, dza_ref, dzx_ref, dc_ref, head_ref, sums_ref):
    batches = 2
    toks = la_ref.shape[0] // batches
    lanes = la_ref.shape[1]
    start = s_ref[ME] * toks
    lam = vec_ref[7:8]
    acc = [jnp.zeros((1, lanes), F32) for _ in range(3)]
    for m in range(batches):
        own = slice(m * toks, (m + 1) * toks)
        q = la_ref[own] + lp_ref[own] * carry_of(s_ref, all_ref, m, True)
        rows = lax.broadcasted_iota(jnp.int32, (toks, lanes), 0)
        keep = (start + rows != s_ref[m]).astype(F32)
        hprev = jnp.where(rows == 0, carry_ref[m : m + 1], jnp.roll(h_ref[own], 1, axis=0))
        rate = r_ref[own]
        gate = i_ref[own]
        c = c_ref[own].astype(F32)
        la = -lam * rate
        root = jnp.sqrt(neg_expm1(2.0 * la))
        decay = jnp.exp(la)
        scaled = keep * root + (1.0 - keep)
        dla = q * hprev * keep * decay - q * keep * gate * c * (decay * decay / root)
        dza = (dla * (-lam) * rate * (1.0 - rate)).astype(BF16)
        dc0 = q * scaled * gate
        dzx = (dc0 * c * (1.0 - gate)).astype(BF16)
        dza_ref[own] = dza
        dzx_ref[own] = dzx
        dc = dc0 + mm_nt(dza, wr_ref[...]) + mm_nt(dzx, wi_ref[...])
        dc_ref[own] = dc
        head_ref[m] = dc[0:8]
        acc[0] += jnp.sum(dza.astype(F32), axis=0, keepdims=True)
        acc[1] += jnp.sum(dzx.astype(F32), axis=0, keepdims=True)
        acc[2] += jnp.sum(dla * rate, axis=0, keepdims=True)
    sums_ref[...] = jnp.zeros_like(sums_ref)
    sums_ref[0:1] = acc[0]
    sums_ref[1:2] = acc[1]
    sums_ref[2:3] = -acc[2] * vec_ref[8:9]


def conv_bwd_kernel(s_ref, dc_ref, head_ref, vb_ref, yb_ref, dyb_ref, vec_ref, w_ref,
                    dvb_ref, keep_ref, swap_ref, sums_ref):
    batches = 2
    ext = vb_ref.shape[0] // batches
    toks = ext - HALO
    lanes = vb_ref.shape[1]
    start = s_ref[ME] * toks
    acc = [jnp.zeros((1, lanes), F32) for _ in range(5)]
    products = []
    for m in range(batches):
        own = slice(m * toks, (m + 1) * toks)
        vb = vb_ref[m * ext : (m + 1) * ext]
        dc = dc_ref[own]
        longer = jnp.concatenate([dc, head_ref[m]], axis=0)
        place = start + lax.broadcasted_iota(jnp.int32, dc.shape, 0)
        place_long = start + lax.broadcasted_iota(jnp.int32, longer.shape, 0)
        dvb = jnp.zeros(dc.shape, F32)
        for k in range(4):
            masked = jnp.where(conv_mask(place_long, s_ref[m], k), longer, 0.0)
            dvb = dvb + vec_ref[k : k + 1] * rolled(masked, -k)[:toks]
            prior = rolled(vb, k)[HALO:]
            acc[k] += jnp.sum(jnp.where(conv_mask(place, s_ref[m], k), dc * prior, 0.0), axis=0, keepdims=True)
        acc[4] += jnp.sum(dc, axis=0, keepdims=True)
        dvb16 = dvb.astype(BF16)
        dvb_ref[own] = dvb16
        products.append(dvb16.astype(F32) * vb[HALO:] + dyb_ref[own].astype(F32) * yb_ref[own])
    sums_ref[...] = jnp.zeros_like(sums_ref)
    for k in range(5):
        sums_ref[k : k + 1] = acc[k]
    side = inner_rows(jnp.concatenate(products, axis=0))
    width = keep_ref.shape[2]
    total = batches * toks
    for r, mine, other in chunk_places(s_ref):
        for ref, block in ((swap_ref, other), (keep_ref, mine)):
            here = lane_block(block, width)
            got = mm(dyb_ref[...], w_ref[:lanes, here]) + mm(dvb_ref[...], w_ref[lanes : 2 * lanes, here])
            ref[r, :total] = got.astype(BF16)
            ref[r, total:] = side


def dp_pairs(along_x, by):
    pairs = []
    for y in range(SIDE):
        for x in range(SIDE):
            there = (y * SIDE + (x + by) % SIDE) if along_x else ((y + by) % SIDE * SIDE + x)
            pairs.append((y * SIDE + x, there))
    return pairs


def send(value, along_x, by):
    return lax.ppermute(value, "dp", dp_pairs(along_x, by))


def send_z(value, by):
    return lax.ppermute(value, "mp", [(z * 2 + c, (z + by) % SIDE * 2 + c) for z in range(SIDE) for c in range(2)])


def swap_cores(value):
    return lax.ppermute(value, "mp", [(i, i ^ 1) for i in range(2 * SIDE)])


def relay(value):
    pairs = [(z * 2 + c, (z + (1, -1)[c]) % SIDE * 2 + c) for z in range(SIDE) for c in range(2)]
    return lax.ppermute(value, "mp", pairs)


def gather_mp(value, core):
    low, high = send_z(value, 1), send_z(value, -1)
    three = jnp.stack([value, low, high])
    far = relay(jnp.where(core == 0, low, high))
    return three, far, swap_cores(three), swap_cores(far)


def reduce_mp(keep, swap, core):
    both = keep.astype(F32) + swap_cores(swap).astype(F32)
    passed = relay(both[2].astype(BF16)).astype(F32)
    low = send_z((both[1] + jnp.where(core == 0, passed, 0.0)).astype(BF16), 1)
    high = send_z((both[3] + jnp.where(core == 1, passed, 0.0)).astype(BF16), -1)
    return both[0], low, high


def exchange_z(chunks):
    lines = [[z * 2 + c for z in range(SIDE)] for c in range(2)]
    return lax.all_to_all(chunks, "mp", 0, 0, axis_index_groups=lines, tiled=True)


def exchange(chunks, axis):
    return lax.all_to_all(chunks, axis, 0, 0, tiled=True)


def to_all(value, axis):
    return exchange(jnp.broadcast_to(value[None], (lax.axis_size(axis),) + value.shape), axis)


def inner_column(rows):
    flat = rows.T
    return flat[:, 0:1] + flat[:, 1:2]


def dn2_sum_kernel(got_ref, rho_ref, dn2_ref, inner_ref, many_ref):
    toks = dn2_ref.shape[0]
    total = got_ref[0].astype(F32)
    for j in range(1, got_ref.shape[0]):
        total = total + got_ref[j].astype(F32)
    dn2_ref[...] = total[:toks]
    inner_ref[...] = inner_column(total[toks:]) / rho_ref[...]
    low = total[:toks].astype(BF16)
    for j in range(many_ref.shape[0]):
        many_ref[j] = low


def finish_kernel(both_ref, low_ref, high_ref, x_ref, cot_ref, x2_ref, dn2_ref, rho1_ref, rho2_ref, inner2_ref,
                  gains_ref, conv_ref, gate_ref, grad_ref, pack_ref, *, batches, full):
    total, width = x_ref.shape
    toks = total // batches
    ext = rho1_ref.shape[0] // batches
    got = both_ref[...] + low_ref[...].astype(F32) + high_ref[...].astype(F32)
    dn1, dn2, x2 = got[:total], dn2_ref[...], x2_ref[...]
    x = x_ref[...].astype(F32)
    rho1 = jnp.concatenate([rho1_ref[m * ext + HALO : (m + 1) * ext] for m in range(batches)], axis=0)
    rho2 = rho2_ref[...]
    inner1 = inner_column(got[total:]) / rho1
    gx2 = (cot_ref[...].astype(F32) + rho2 * gains_ref[1:2] * dn2
           - x2 * (rho2 * rho2 * rho2 / full * inner2_ref[...]))
    grad_ref[...] = gx2 + rho1 * gains_ref[0:1] * dn1 - x * (rho1 * rho1 * rho1 / full * inner1)
    gain_grads = (jnp.sum(dn1 * x * rho1, axis=0, keepdims=True), jnp.sum(dn2 * x2 * rho2, axis=0, keepdims=True))
    pack_ref[...] = jnp.zeros_like(pack_ref)
    deep = pack_ref.shape[0]
    sums = jnp.concatenate([conv_ref[:5], gate_ref[:3]], axis=0)
    size = sums.shape[1] // 2
    for i in range(deep):
        few = size // deep
        for j in range(2):
            at = j * size + i * few
            pack_ref[i, 8 * j : 8 * j + 8, :few] = sums[:, at : at + few]
        for k, row in enumerate(gain_grads):
            pack_ref[i, 16 + k : 17 + k, : width // deep] = row[:, i * (width // deep) : (i + 1) * (width // deep)]


def small_out_kernel(got_ref, taps_ref, shift_ref, rate_ref, input_ref, decay_ref, one_ref, two_ref):
    total = got_ref[0]
    for i in range(1, got_ref.shape[0]):
        total = total + got_ref[i]
    few = shift_ref.shape[1]
    for j in range(2):
        for k in range(4):
            taps_ref[k, j : j + 1, :] = total[8 * j + k : 8 * j + k + 1, :few]
        for k, ref in enumerate((shift_ref, rate_ref, input_ref, decay_ref)):
            ref[j : j + 1, :] = total[8 * j + 4 + k : 8 * j + 5 + k, :few]
    one_ref[...] = total[16:17, : one_ref.shape[1]]
    two_ref[...] = total[17:18, : two_ref.shape[1]]


def late_kernel(dvb_ref, n1_ref, c_ref, dza_ref, dzx_ref, out_ref):
    deep, _, rows = out_ref.shape
    lanes = dvb_ref.shape[1]
    size = lanes // 2
    few = size // deep
    for i in range(0, deep, SIDE):
        got = mm_tn(dvb_ref[...], n1_ref[:, i * rows : (i + SIDE) * rows]).astype(BF16)
        for d in range(SIDE):
            out_ref[i + d, :lanes] = got[:, d * rows : (d + 1) * rows]
    out_ref[:, lanes:] = jnp.zeros((deep, out_ref.shape[1] - lanes, rows), BF16)
    for kind, ref in enumerate((dza_ref, dzx_ref)):
        both = mm_tn(c_ref[...], ref[...])
        for j in range(2):
            k = 2 * kind + j
            block = both[j * size : (j + 1) * size, j * size : (j + 1) * size].astype(BF16)
            for i in range(deep):
                part = block[i * few : (i + 1) * few]
                out_ref[i, lanes + 16 * k : lanes + 16 * k + few] = part[:, :rows]
                at = lanes + 64 + 16 * (k // 2)
                here = slice(64 * (k % 2), 64 * (k % 2) + size - rows)
                out_ref[i, at : at + few, here] = part[:, rows:]


def late_out_kernel(got_ref, value_ref, rate_ref, input_ref):
    lanes, rows = value_ref.shape
    few, _, size = rate_ref.shape
    total = got_ref[0].astype(F32)
    for i in range(1, got_ref.shape[0]):
        total = total + got_ref[i].astype(F32)
    value_ref[...] = total[:lanes]
    for kind, ref in enumerate((rate_ref, input_ref)):
        for j in range(2):
            k = 2 * kind + j
            at = lanes + 16 * k
            ref[:, j, :rows] = total[at : at + few]
            at = lanes + 64 + 16 * (k // 2)
            ref[:, j, rows:] = total[at : at + few, 64 * (k % 2) : 64 * (k % 2) + size - rows]


def early_out_kernel(got_ref, out_ref, branch_ref):
    lanes = out_ref.shape[0]
    out_ref[...] = got_ref[:lanes].astype(F32)
    branch_ref[...] = got_ref[lanes:].astype(F32)


def beside(at):
    return at + 1 - 2 * (at % 2)


def across(at):
    return SIDE - 1 - at


def send_to(value, along_x, partner):
    pairs = []
    for y in range(SIDE):
        for x in range(SIDE):
            there = (y * SIDE + partner(x)) if along_x else (partner(y) * SIDE + x)
            pairs.append((y * SIDE + x, there))
    return lax.ppermute(value, "dp", pairs)


def at_of(s_ref, along_x):
    return s_ref[COL_X if along_x else ROW_Y]


def partners_of(one_set):
    return (beside, across) if one_set[3] is beside else (across, beside)


def whole_spec(dims):
    return pl.BlockSpec(dims, lambda i: (0,) * len(dims))


def half_spec(units, wide, index):
    return pl.BlockSpec((units, wide), lambda i: (0, index))


def call_whole(name, kernel, outs, args, specs=None, scratch=(), ties=()):
    ins = [SCALARS if v.dtype == jnp.int32 else whole_spec(v.shape) for v in args]
    for k, spec in (specs or {}).items():
        ins[k] = spec
    return call(kernel, outs, ins, args, grid=(1,), out_specs=[whole_spec(o.shape) for o in outs], scratch=scratch,
                name=name, ties=ties)


def halving_one(name, scalars, group, wide, ties=()):
    operands, sets = group

    def kernel(s_ref, *refs):
        ins, outs = refs[: len(operands)], refs[len(operands) :]
        for one_set, out_ref in zip(sets, outs):
            first, second = partners_of(one_set)
            there = first(at_of(s_ref, one_set[2]))
            out_ref[:, :wide] = one_set[0](ins, there).astype(BF16)
            out_ref[:, wide:] = one_set[0](ins, second(there)).astype(BF16)

    outs = [shape((t[1], 2 * wide), BF16) for t in sets]
    sent = call_whole(name, kernel, outs, (scalars, *operands), ties=ties)
    return sent, [send_to(v, t[2], partners_of(t)[0]) for v, t in zip(sent, sets)]


def halving_two(name, scalars, group, wide, got, ties=()):
    operands, sets = group

    def kernel(s_ref, *refs):
        ins, got, outs = refs[: len(operands)], refs[len(operands) : -len(sets)], refs[-len(sets) :]
        for one_set, got_ref, out_ref in zip(sets, got, outs):
            there = partners_of(one_set)[1](at_of(s_ref, one_set[2]))
            out_ref[...] = (one_set[0](ins, there) + got_ref[...].astype(F32)).astype(BF16)

    outs = [shape((t[1], wide), BF16) for t in sets]
    specs = {1 + len(operands) + k: half_spec(t[1], wide, 1) for k, t in enumerate(sets)}
    sent = call_whole(name, kernel, outs, (scalars, *operands, *got), specs, ties=ties)
    return sent, [send_to(v, t[2], partners_of(t)[1]) for v, t in zip(sent, sets)]


def halving_three(name, scalars, group, wide, got_one, got_two, ties=()):
    size = wide // SIDE
    operands, sets = group
    tall = [sum(t[1] for t in sets if t[2] == along_x) for along_x in (False, True)]
    count = len(operands)

    def kernel(s_ref, *refs):
        ins, ones, twos = refs[:count], refs[count : count + len(sets)], refs[count + len(sets) : -2 * SIDE - 1]
        outs, held = refs[-2 * SIDE - 1 : -1], refs[-1]
        start = [0, 0]
        for (chunk, units, along_x, _), one, two in zip(sets, ones, twos):
            held[:units] = chunk(ins, at_of(s_ref, along_x)) + one[...].astype(F32) + two[...].astype(F32)
            here = slice(start[along_x], start[along_x] + units)
            start[along_x] += units
            for d in range(SIDE):
                ref = outs[SIDE * along_x + d]
                at = (at_of(s_ref, not along_x) + d) % SIDE
                ref[here] = held[:units, lane_block(at, size)].astype(ref.dtype)

    outs = [shape((tall[k], size), BF16 if d else F32) for k in range(2) for d in range(SIDE)]
    specs = {1 + count + k: half_spec(t[1], wide, 0) for k, t in enumerate(sets)}
    parts = call_whole(name, kernel, outs, (scalars, *operands, *got_one, *got_two), specs,
                       [pltpu.VMEM((max(t[1] for t in sets), wide), F32)], ties)
    return [parts[SIDE * k + d] if d == 0 else send(parts[SIDE * k + d], not k, d) for k in range(2) for d in range(SIDE)]


def block_diagonal(blocks):
    count, size = blocks.shape[0], blocks.shape[1]
    rows = [jnp.pad(blocks[j], ((0, 0), (j * size, (count - 1 - j) * size))) for j in range(count)]
    return jnp.concatenate(rows, axis=0)


def body(inputs, cotangent, row_split, first_gain, branch_weight, value_weight, conv_weight, conv_bias,
         rate_blocks, input_blocks, rate_bias, input_bias, decay_param, out_weight, second_gain,
         gate_weight, up_weight, down_weight):
    batches, toks, width = inputs.shape
    parts = lax.axis_size("mp")
    deep = lax.axis_size("dp")
    full = width * parts
    blocks, size = rate_blocks.shape[0], rate_blocks.shape[1]
    lanes = blocks * size
    rows = branch_weight.shape[0]
    units = gate_weight.shape[1]
    total = batches * toks
    ext = toks + HALO
    me = lax.axis_index("dp")
    at_mp = lax.axis_index("mp")
    core = at_mp % 2
    scalars = jnp.concatenate(
        [row_split, jnp.stack([me, me // SIDE, me % SIDE, at_mp // 2, core, jnp.zeros_like(me)])]).astype(jnp.int32)

    w_rec = lax.all_gather(jnp.concatenate([branch_weight.T, value_weight.T, out_weight], axis=0), "dp")
    w_ffn = lax.all_gather(jnp.stack([gate_weight, up_weight, down_weight.T]), "dp")

    decay = decay_param.reshape(1, lanes).astype(F32)
    vectors = jnp.concatenate(
        [conv_weight.reshape(4, lanes).astype(F32), conv_bias.reshape(1, lanes).astype(F32),
         rate_bias.reshape(1, lanes).astype(F32), input_bias.reshape(1, lanes).astype(F32),
         8.0 * jax.nn.softplus(decay), 8.0 * jax.nn.sigmoid(decay), jnp.zeros((7, lanes), F32)], axis=0)
    rate_mat = block_diagonal(rate_blocks)
    input_mat = block_diagonal(input_blocks)

    pairs = [(i, i + 1) for i in range(deep - 1)]
    before = lax.ppermute(inputs[:, toks - HALO :], "dp", pairs)
    gains = jnp.concatenate([first_gain[None], second_gain[None], jnp.zeros((HALO - 2, width), BF16)], axis=0)
    payload = jnp.concatenate([jnp.concatenate([before, inputs], axis=1).reshape(batches * ext, width), gains], axis=0)
    x_parts = gather_mp(payload, core)
    n1, n1_own, rho1, gain_rows = call(
        norm_one_kernel,
        [shape((batches * ext, full), BF16), shape((total, full), BF16), shape((batches * ext, 1)), shape((HALO, full))],
        [SCALARS] + [WHOLE] * 4, (scalars, *x_parts),
        scratch=[pltpu.VMEM((batches * ext, full), BF16)], name="norm_one")
    cot_parts = gather_mp(cotangent.reshape(total, width), core)

    grown = shape((total, lanes))

    def full_spec(dims):
        return pl.BlockSpec(dims, lambda i: (0,) * len(dims))

    w_rec, yb, vb, c, rate, gate, a, prod, state, last = call(
        rec_fwd_kernel,
        [shape((3 * lanes, full), BF16), grown, shape((batches * ext, lanes)), shape((total, lanes), BF16)]
        + [grown] * 5 + [shape((8, lanes))],
        [SCALARS] + [WHOLE] * 5,
        (scalars, n1, w_rec, vectors, rate_mat, input_mat), name="rec_fwd", ties=cot_parts)
    ends = to_all(last, "dp")
    chunk = shape((SIDE, total, width), BF16)
    chunk_long = shape((SIDE, total + HALO, width), BF16)
    def with_weights(kernel, outs, args, w_at, blocks_at, name, ties=()):
        ins = [SCALARS if a.dtype == jnp.int32 else full_spec(a.shape) for a in args]
        ins[w_at] = pl.BlockSpec((blocks_at[1] * lanes, full), lambda i: (blocks_at[0], 0))
        return call(kernel, outs, ins, args, grid=(1,), out_specs=[full_spec(o.shape) for o in outs],
                    name=name, ties=ties)

    h, carry, o, keep, swap = with_weights(
        rec_out_kernel, [grown, shape((8, lanes)), shape((total, lanes), BF16), chunk, chunk],
        (scalars, ends, prod, state, yb, w_rec), 5, (2, 1), "rec_out")
    x_own = inputs.reshape(total, width).astype(F32)
    both, low, high = reduce_mp(keep, swap, core)
    x2 = x_own + (both + low.astype(F32) + high.astype(F32))
    x2_parts = gather_mp(x2.astype(BF16), core)

    steps = 3
    cols = units // steps
    n2, x2_full, rho2, cot_full, hid, dgt, dup, part_o, keep, swap = call(
        ffn_kernel,
        [shape((total, full), BF16)] * 2 + [shape((total, 1)), shape((total, full), BF16)]
        + [shape((total, units), BF16)] * 3
        + [shape((total, full), BF16), chunk_long, chunk_long],
        [SCALARS] + [full_spec(v.shape) for v in x2_parts + cot_parts] + [full_spec(gain_rows.shape),
         pl.BlockSpec((deep, 3, rows, cols), lambda g: (0, 0, 0, g))],
        (scalars, *x2_parts, *cot_parts, gain_rows, w_ffn),
        grid=(steps,),
        out_specs=[full_spec((total, full))] * 2 + [full_spec((total, 1)), full_spec((total, full))]
        + [pl.BlockSpec((total, cols), lambda g: (0, g))] * 3
        + [full_spec((total, full)), full_spec(chunk_long.shape), full_spec(chunk_long.shape)],
        scratch=[pltpu.VMEM((total, full), F32), pltpu.VMEM((total, full), F32), pltpu.VMEM((total, cols), F32)],
        name="ffn")

    def row_lanes(ref, at):
        return ref[:, lane_block(at, SIDE * rows)]

    def column_lanes(ref, at):
        return jnp.concatenate([ref[:, lane_block(y * SIDE + at, rows)] for y in range(SIDE)], axis=1)

    mid, low = units // 2, units // 4

    def ffn_set(along_x, second):
        lanes_of = column_lanes if along_x else row_lanes
        main = slice(second * mid, (second + 1) * mid)
        part = slice((2 * along_x + second) * low, (2 * along_x + second + 1) * low)

        def chunk(refs, at):
            n2_ref, cot_ref, hid_ref = refs[0], refs[1], refs[4]
            grad_ref = refs[3] if along_x else refs[2]
            return jnp.concatenate(
                [mm_tn(grad_ref[:, main], lanes_of(n2_ref, at)), mm_tn(hid_ref[:, part], lanes_of(cot_ref, at))], axis=0)

        return chunk, mid + low, along_x, across if second else beside

    wide = SIDE * rows
    ffn_group = ((n2, cot_full, dgt, dup, hid),
                 [ffn_set(along_x, second) for along_x in (False, True) for second in (False, True)])
    dn2_parts = (keep.astype(F32) + swap_cores(swap).astype(F32)).astype(BF16)
    ffn_one, ffn_got_one = halving_one("ffn_grad_one", scalars, ffn_group, wide, (dn2_parts,))
    layer_part = lax.psum_scatter(part_o, "mp", scatter_dimension=1, tiled=True)
    got = exchange_z(dn2_parts)
    dn2, inner2, dn2_many = call(
        dn2_sum_kernel, [shape((total, width)), shape((total, 1)), shape((SIDE, total, width), BF16)], [WHOLE] * 2,
        (got, rho2), name="dn2_sum", ties=(ffn_one[0],))
    dn2_line = exchange_z(dn2_many)

    gr, dyb, adj, adj_prod, first = with_weights(
        rec_bwd_kernel,
        [shape((total, full), BF16), shape((total, lanes), BF16), grown, grown, shape((deep, 8, lanes))],
        (scalars, dn2_line, swap_cores(dn2_line), x2_full, cot_full, gain_rows, rho2, inner2, w_rec, yb, h, a, prod),
        8, (2, 1), "rec_bwd")

    starts = exchange(first, "dp")

    def early_kernel(o_ref, gr_ref, dyb_ref, n1_ref, out_ref):
        for k, (left, right) in enumerate(((o_ref, gr_ref), (dyb_ref, n1_ref))):
            units_at = slice(k * lanes, (k + 1) * lanes)
            for i in range(0, deep, SIDE):
                got = mm_tn(left[...], right[:, i * rows : (i + SIDE) * rows]).astype(BF16)
                for d in range(SIDE):
                    out_ref[i + d, units_at] = got[:, d * rows : (d + 1) * rows]

    early = call(early_kernel, [shape((deep, 2 * lanes, rows), BF16)], [WHOLE] * 4, (o, gr, dyb, n1_own),
                 name="early_grad", ties=tuple(ffn_got_one))[0]
    ffn_two, ffn_got_two = halving_two("ffn_grad_two", scalars, ffn_group, wide, ffn_got_one, (early,))
    early = lax.psum_scatter(early.reshape(-1, rows), "dp", scatter_dimension=0, tiled=True)

    dza, dzx, dc, head, sums_gate = call(
        gate_bwd_kernel,
        [shape((total, lanes), BF16)] * 2 + [grown, shape((batches, 8, lanes)), shape((8, lanes))],
        [SCALARS] + [WHOLE] * 12,
        (scalars, starts, adj, adj_prod, a, h, carry, c, rate, gate, vectors, rate_mat, input_mat),
        name="gate_bwd", ties=(ffn_two[0],))
    following = lax.ppermute(head, "dp", [(i + 1, i) for i in range(deep - 1)])
    dvb, keep, swap, sums_conv = with_weights(
        conv_bwd_kernel,
        [shape((total, lanes), BF16), chunk_long, chunk_long, shape((8, lanes))],
        (scalars, dc, following, vb, yb, dyb, vectors, w_rec), 7, (0, 2), "conv_bwd")
    late = call(late_kernel, [shape((deep, lanes + 96, rows), BF16)], [WHOLE] * 5, (dvb, n1_own, c, dza, dzx),
                name="late_grad", ties=tuple(ffn_got_two))[0]
    keep, late = lax.optimization_barrier((keep, late))
    late_got = exchange(late, "dp")
    both, below, above = reduce_mp(keep, swap, core)
    grad_sums = halving_three("ffn_grad_three", scalars, ffn_group, wide, ffn_got_one, ffn_got_two, (late,))
    layer_out = (x2 + layer_part.astype(F32)).astype(BF16)
    small_gains = jnp.stack([first_gain, second_gain]).astype(F32)
    input_grad, pack = call(
        functools.partial(finish_kernel, batches=batches, full=full),
        [shape((total, width)), shape((deep, 24, rows))], [WHOLE] * 13,
        (both, below, above, inputs.reshape(total, width), cotangent.reshape(total, width), x2, dn2, rho1, rho2, inner2,
         small_gains, sums_conv, sums_gate), name="finish")
    few = size // deep
    pair = shape((blocks, few))
    pack, late_got = lax.optimization_barrier((pack, late_got))
    value_grad, rate_g, input_g = call(
        late_out_kernel, [shape((lanes, rows))] + [shape((few, blocks, size))] * 2, [WHOLE], (late_got,),
        name="late_out")
    taps, shift, rate_b, input_b, decay_g, gain_a, gain_b = call(
        small_out_kernel, [shape((4, blocks, few)), pair, pair, pair, pair] + [shape((1, width // deep))] * 2, [WHOLE],
        (exchange(pack, "dp"),), name="small_out")
    out_grad, branch_grad = call(early_out_kernel, [shape((lanes, rows))] * 2, [WHOLE], (early,), name="early_out")

    def ffn_out_kernel(*refs):
        outs = refs[2 * SIDE :]
        for k in range(2):
            for second in range(2):
                at = second * (mid + low)
                sums = [sum(ref[there].astype(F32) for ref in refs[SIDE * k : SIDE * k + SIDE])
                        for there in (slice(at, at + mid), slice(at + mid, at + mid + low))]
                outs[k][:, second * mid : (second + 1) * mid] = sums[0].T
                outs[2][(2 * k + second) * low : (2 * k + second + 1) * low] = sums[1]

    gate_grad, up_grad, down = call(
        ffn_out_kernel, [shape((rows, units))] * 2 + [shape((units, rows))], [WHOLE] * (2 * SIDE),
        grad_sums, name="ffn_out", ties=(pack, value_grad, out_grad))

    return (
        layer_out.reshape(batches, toks, width), input_grad.reshape(batches, toks, width),
        gain_a.reshape(-1), branch_grad.T, value_grad.T, taps, shift, rate_g.transpose(1, 0, 2),
        input_g.transpose(1, 0, 2), rate_b, input_b, decay_g,
        out_grad, gain_b.reshape(-1), gate_grad, up_grad, down,
    )


def solution(mesh):
    placed = (
        P(None, "dp", "mp"), P(None, "dp", "mp"), P(), P("mp"), P("dp", "mp"), P("dp", "mp"),
        P(None, "mp", None), P("mp", None), P("mp", None, None), P("mp", None, None), P("mp", None),
        P("mp", None), P("mp", None), P("mp", "dp"), P("mp"), P("dp", "mp"), P("dp", "mp"), P("mp", "dp"),
    )
    given = (
        P(None, "dp", "mp"), P(None, "dp", "mp"), P(("mp", "dp")), P("dp", "mp"), P("dp", "mp"),
        P(None, "mp", "dp"), P("mp", "dp"), P("mp", "dp", None), P("mp", "dp", None), P("mp", "dp"),
        P("mp", "dp"), P("mp", "dp"), P("mp", "dp"), P(("mp", "dp")), P("dp", "mp"), P("dp", "mp"), P("mp", "dp"),
    )
    return jax.shard_map(body, mesh=mesh, in_specs=placed, out_specs=given, check_vma=False)
```

time: 2280 us -> 330 us (0.14)
  waiting for transfers between devices: 1100 us -> 97.8 us
  local copies, waits for them, and re-layouts: 519 us -> 12.7 us
  blocking collectives: 374 us -> 29.5 us
  other arithmetic: 168 us -> 10.4 us
  Pallas kernels: 0 us -> 81.7 us
  matrix products: 68.8 us -> 0 us
  starting transfers between devices: 11.5 us -> 78.3 us
    unnamed x36 -> x4, waiting for transfers between devices: 558 us -> 0.07 us
    reduce_scatter x12 -> x2, waiting for transfers between devices: 416 us -> 0.01 us  [the longest x1 0.01 us: body(): layer_part = lax.psum_scatter(part_o, 'mp', scatter_dimension=1, tiled=True)]
    all_gather x14 -> x0, blocking collectives: 245 us -> none  [the longest x6 137 us: carried_in(): pieces = jax.tree.map(lambda part: lax.all_gather(part, axis), value)]
    slice x163 -> x1, local copies, waits for them, and re-layouts: 242 us -> 0.01 us  [body(): before = lax.ppermute(inputs[:, toks - HALO:], 'dp', pairs)]
    pad x96 -> x0, local copies, waits for them, and re-layouts: 181 us -> none  [the longest x48 115 us: body(): lax.associative_scan(link, (decay_factor, drive_term))]
    pallas_call x0 -> x18, Pallas kernels: none -> 81.7 us  [call(): pl.pallas_call(kernel, out_shape=outs, in_specs=ins, out_specs=out_specs...]
    all_gather x6 -> x2, waiting for transfers between devices: 116 us -> 39.2 us  [the longest x1 22.8 us: body(): lax.all_gather(jnp.concatenate([branch_weight.T, value_weight.T, out_weig...]
    unnamed x1 -> x0, blocking collectives: 74.3 us -> none
  transfers between devices with their start and end apart: 31 -> 49, of which waited for: 24 -> 25; matrix products, arithmetic and copies ran while one was open for 21% -> 4% of each run, Pallas kernels for 0% -> 20%
where the time goes in v1:
time: 330 us; the launch traced here: 325 us
  waiting for transfers between devices  97.8 us (30%)
  Pallas kernels  81.7 us (25%)
  starting transfers between devices  78.3 us (24%)
  blocking collectives  29.5 us (9%)
  between operations  14.7 us (4%)
  local copies, waits for them, and re-layouts  12.7 us (4%)
  other arithmetic  10.4 us (3%)
    pallas_call x18, Pallas kernels, call(): pl.pallas_call(kernel, out_shape=outs, in_specs=ins, out_specs=out_specs...  81.7 us
    all_gather x1, waiting for transfers between devices, body(): lax.all_gather(jnp.concatenate([branch_weight.T, value_weight.T, out_weig...  22.8 us
    all_to_all x3, starting transfers between devices, exchange(): return lax.all_to_all(chunks, axis, 0, 0, tiled=True)  22.4 us
    ppermute x10, starting transfers between devices, send_z(): lax.ppermute(value, 'mp', [(z * 2 + c, (z + by) % SIDE * 2 + c) for z in...  17.1 us
    all_gather x1, waiting for transfers between devices, body(): lax.all_gather(jnp.stack([gate_weight, up_weight, down_weight.T]), 'dp')  16.3 us
    ppermute x10, waiting for transfers between devices, send_z(): lax.ppermute(value, 'mp', [(z * 2 + c, (z + by) % SIDE * 2 + c) for z in...  16.2 us
    all_to_all x1, blocking collectives, exchange(): return lax.all_to_all(chunks, axis, 0, 0, tiled=True)  16.1 us
    ppermute x6, starting transfers between devices, send(): return lax.ppermute(value, 'dp', dp_pairs(along_x, by))  13.8 us
  transfers between devices with their start and end apart: 49, of which 25 were waited for; matrix products, arithmetic and copies ran while one was open for 4% of the time, Pallas kernels for 20%

profile of v1, /device:TPU:0, one launch (start us, length us, event | category | flops | bytes accessed | tf_op | source)
XLA Modules:
  0.0 325.2 jit_solution(16934509657346665604)
XLA Ops:
  11.4 4.2 %collective-permute-start.7 = (bf16[256,256]{1,0:T(8,128)(2,1)S(1)}, bf16[256,256]{1,0:T(8,128)(2,1)S(1)}, u32[]{:S(2)}, u32[]{:S(2)}) collective-permute-start(bf16[256,256]{1,0:T(8,128)(2,1)S(1)} %bitcast.92), channel_id=1, source_target_pairs={{0,6},{1,7},{2,0},{3,1},{4,2},{5,3},{6,4},{7,5},{8,14},{9,15},{10,... | collective-permute-start | bytes 393224 | tf_op jit(solution)/shard_map/ppermute | solution.py:440
  15.6 3.4 %collective-permute-start = (bf16[2,16,256]{2,1,0:T(8,128)(2,1)S(1)}, bf16[2,16,256]{2,1,0:T(8,128)(2,1)S(1)}, u32[]{:S(2)}, u32[]{:S(2)}) collective-permute-start(bf16[2,16,256]{2,1,0:T(8,128)(2,1)S(1)} %slice.41), channel_id=1, source_target_pairs={{0,8},{8,16},{16,24},{24,32},{32,40},{40,48},{48,56},{56,64},{64,7... | collective-permute-start | bytes 49160 | tf_op jit(solution)/shard_map/ppermute | solution.py:719
  20.6 3.3 %collective-permute-start.2 = (bf16[304,256]{1,0:T(8,128)(2,1)S(1)}, bf16[304,256]{1,0:T(8,128)(2,1)S(1)}, u32[]{:S(2)}, u32[]{:S(2)}) collective-permute-start(bf16[304,256]{1,0:T(8,128)(2,1)S(1)} %maximum_maximum_fusion), channel_id=1, source_target_pairs={{0,6},{1,7},{2,0},{3,1},{4,2},{5,3},{6,4},{7,5},{8,14},{9,15},{10,... | collective-permute-start | bytes 466952 | tf_op jit(solution)/shard_map/ppermute | solution.py:440
  24.0 3.0 collective-permute-done.1
  30.9 2.7 collective-permute-done.3.far
  38.9 3.5 %norm_one.1 = (bf16[288,2048]{1,0:T(8,128)(2,1)}, bf16[256,2048]{1,0:T(8,128)(2,1)}, f32[288,1]{1,0:T(8,128)}, f32[16,2048]{1,0:T(8,128)}) custom-call(s32[8]{0:T(128)} %concatenate.21.s_ref.refs_0_, bf16[3,304,256]{2,1,0:T(8,128)(2,1)} %copy-done.14, bf16[304,256]{1,0:T(8,128)(2,1)} %copy-done.40, bf16[3,304,256]{2,1,0:T(8,128)(2,1)} %copy-done.31, ...), custom_call_target="tpu_custom_call" | custom-call | flops 4024999936 | tf_op jit(solution)/shard_map/norm_one/pallas_call | solution.py:106
  42.5 22.8 %all-gather.5.cloned.1.call-done = bf16[16896,128]{1,0:T(8,128)(2,1)} async-done(((bf16[1056,128]{1,0:T(8,128)(2,1)}), bf16[16896,128]{1,0:T(8,128)(2,1)}) %all-gather.5.cloned.1.call-update) | async-done | bytes 4325392 | tf_op jit(solution)/shard_map/all_gather | solution.py:707
  65.3 8.3 %rec_fwd.1 = (bf16[1056,2048]{1,0:T(8,128)(2,1)}, f32[256,352]{1,0:T(8,128)}, f32[288,352]{1,0:T(8,128)}, bf16[256,352]{1,0:T(8,128)(2,1)}, f32[256,352]{1,0:T(8...) custom-call(s32[8]{0:T(128)} %concatenate.21.s_ref.refs_0_, ...), custom_call_target="tpu_custom_call" | custom-call | flops 9660000256 | tf_op jit(solution)/shard_map/rec_fwd/pallas_call | solution.py:106
  74.4 16.1 %all_to_all.30.all_ref = f32[16,8,352]{2,1,0:T(8,128)} all-to-all(f32[16,8,352]{2,1,0:T(8,128)S(1)} %broadcast_in_dim.32), channel_id=1, replica_groups=mesh['dp'=16,'mp'=8] {'dp'}, dimensions={0} | all-to-all | bytes 360448 | tf_op jit(solution)/shard_map/all_to_all | solution.py:473
  90.5 3.7 %rec_out.1 = (f32[256,352]{1,0:T(8,128)}, f32[8,352]{1,0:T(8,128)}, bf16[256,352]{1,0:T(8,128)(2,1)}, bf16[4,256,256]{2,1,0:T(8,128)(2,1)}, bf16[4,256,256]{2,1,0:T(8,128)(2,1)}) custom-call(s32[8]{0:T(128)} %concatenate.21.s_ref.refs_0_, f32[16,8,352]{2,1,0:T(8,128)} %all_to_all.30.all_ref, f32[256,352]{1,0:T(8,128)} %get-tuple-element.102.pr_ref, ...), custom_call_target="tpu_custom_call" | custom-call | flops 4255000064 | tf_op jit(solution)/shard_map/rec_out/pallas_call | solution.py:106
  94.1 2.1 collective-permute-done.11
  99.1 4.6 %collective-permute-done.12 = bf16[256,256]{1,0:T(8,128)(2,1)S(1)} collective-permute-done((bf16[256,256]{1,0:T(8,128)(2,1)S(1)}, bf16[256,256]{1,0:T(8,128)(2,1)S(1)}, u32[]{:S(2)}, u32[]{:S(2)}) %collective-permute-start.12) | collective-permute-done | bytes 131104 | tf_op jit(solution)/shard_map/ppermute | solution.py:449
  104.2 2.9 collective-permute-start.14
  107.1 2.9 collective-permute-done.13
  110.8 3.2 collective-permute-start.16
  114.3 2.3 collective-permute-done.16
  116.6 3.9 %collective-permute-done.15 = bf16[256,256]{1,0:T(8,128)(2,1)S(1)} collective-permute-done((bf16[256,256]{1,0:T(8,128)(2,1)S(1)}, bf16[256,256]{1,0:T(8,128)(2,1)S(1)}, u32[]{:S(2)}, u32[]{:S(2)}) %collective-permute-start.15) | collective-permute-done | bytes 131104 | tf_op jit(solution)/shard_map/ppermute | solution.py:440
  120.7 6.2 %collective-permute-done.17.far = bf16[256,256]{1,0:T(8,128)(2,1)S(1)} collective-permute-done((bf16[256,256]{1,0:T(8,128)(2,1)S(1)}, bf16[256,256]{1,0:T(8,128)(2,1)S(1)}, u32[]{:S(2)}, u32[]{:S(2)}) %collective-permute-start.17) | collective-permute-done | bytes 131104 | tf_op jit(solution)/shard_map/ppermute | solution.py:449
  128.2 16.3 %all-gather.7.cloned.1.call-done = bf16[48,128,768]{2,1,0:T(8,128)(2,1)} async-done(((bf16[3,128,768]{2,1,0:T(8,128)(2,1)}), bf16[48,128,768]{2,1,0:T(8,128)(2,1)}) %all-gather.7.cloned.1.call-update) | async-done | bytes 9437200 | tf_op jit(solution)/shard_map/all_gather | solution.py:708
  144.6 13.1 %ffn.1 = (bf16[256,2048]{1,0:T(8,128)(2,1)}, bf16[256,2048]{1,0:T(8,128)(2,1)}, f32[256,1]{1,0:T(8,128)}, bf16[256,2048]{1,0:T(8,128)(2,1)}, bf16[256,768]{1,0:T...) custom-call(s32[8]{0:T(128)} %concatenate.21.s_ref.refs_0_, ...), custom_call_target="tpu_custom_call" | custom-call | flops 14835000320 | tf_op jit(solution)/shard_map/ffn/pallas_call | solution.py:106
  157.8 2.1 collective-permute-done.20
  160.9 4.4 %all-to-all-start.1 = ((bf16[4,272,256]{2,1,0:T(8,128)(2,1)}), bf16[4,272,256]{2,1,0:T(8,128)(2,1)}, u32[]{:S(2)}, u32[]{:S(2)}) async-start(bf16[4,272,256]{2,1,0:T(8,128)(2,1)} %add_convert_fusion.refs_6_), calls=%async_computation.2 | async-start | bytes 1114112 | tf_op jit(solution)/shard_map/all_to_all | solution.py:469
  165.3 5.2 %ffn_grad_one.1 = (bf16[576,1024]{1,0:T(8,128)(2,1)}, bf16[576,1024]{1,0:T(8,128)(2,1)}, bf16[576,1024]{1,0:T(8,128)(2,1)}, bf16[576,1024]{1,0:T(8,128)(2,1)}) custom-call(s32[8]{0:T(128)} %concatenate.21.s_ref.refs_0_, bf16[256,2048]{1,0:T(8,128)(2,1)} %get-tuple-element.113.refs_1_, bf16[256,2048]{1,0:T(8,128)(2,1)} %get-tuple-element.114.refs_2_.cotf_ref, ...), custom_call_target="tpu_custom_call" | custom-call | flops 5750000128 | tf_op jit(solution)/shard_map/ffn_grad_one/pallas_call | solution.py:106
  170.5 2.7 collective-permute-start.23
  177.5 2.2 dn2_sum.1
  179.7 13.4 %all_to_all.31.dn2_ref = bf16[4,256,256]{2,1,0:T(8,128)(2,1)S(1)} all-to-all(bf16[4,256,256]{2,1,0:T(8,128)(2,1)} %get-tuple-element.119), channel_id=1, replica_groups={{0,2,4,6},{1,3,5,7},{8,10,12,14},{9,11,13,15},{16,18,20,22},{17,19,21,2..., dimensions={0} | all-to-all | bytes 1048576 | tf_op jit(solution)/shard_map/all_to_all | solution.py:469
  195.8 6.0 %rec_bwd.1 = (bf16[256,2048]{1,0:T(8,128)(2,1)}, bf16[256,352]{1,0:T(8,128)(2,1)}, f32[256,352]{1,0:T(8,128)}, f32[256,352]{1,0:T(8,128)}, f32[16,8,352]{2,1,0:T(8,128)}) custom-call(s32[8]{0:T(128)} %concatenate.21.s_ref.refs_0_, bf16[4,256,256]{2,1,0:T(8,128)(2,1)} %copy-done.3, bf16[4,256,256]{2,1,0:T(8,128)(2,1)} %copy-done.13, ...), custom_call_target="tpu_custom_call" | custom-call | flops 345000000 | tf_op jit(solution)/shard_map/rec_bwd/pallas_call | solution.py:106
  203.8 4.2 %early_grad.1.refs_10_ = bf16[16,704,128]{2,1,0:T(8,128)(2,1)} custom-call(bf16[256,352]{1,0:T(8,128)(2,1)} %get-tuple-element.134.refs_0_, bf16[256,2048]{1,0:T(8,128)(2,1)} %get-tuple-element.135.refs_1_, bf16[256,352]{1,0:T(8,128)(2,1)} %get-tuple-element.136.refs_2_.dyb_ref, bf16[256,2048]{1,0:T(8,128)(2,1)} %get-tuple-element.137.refs_3_.refs_1_, ...), custom_call_target="tpu_custom_call" | custom-call | flops 345000000 | tf_op jit(solution)/shard_map/early_grad/pallas_call | solution.py:106
  208.0 14.0 %all-to-all-start.3 = ((f32[16,8,352]{2,1,0:T(8,128)}), f32[16,8,352]{2,1,0:T(8,128)S(1)}, u32[]{:S(2)}, u32[]{:S(2)}) async-start(f32[16,8,352]{2,1,0:T(8,128)} %get-tuple-element.124), calls=%async_computation.4 | async-start | bytes 393216 | tf_op jit(solution)/shard_map/all_to_all | solution.py:473
  222.0 4.5 %ffn_grad_two.1 = (bf16[576,512]{1,0:T(8,128)(2,1)}, bf16[576,512]{1,0:T(8,128)(2,1)}, bf16[576,512]{1,0:T(8,128)(2,1)}, bf16[576,512]{1,0:T(8,128)(2,1)}) custom-call(s32[8]{0:T(128)} %concatenate.21.s_ref.refs_0_, bf16[256,2048]{1,0:T(8,128)(2,1)} %get-tuple-element.113.refs_1_, bf16[256,2048]{1,0:T(8,128)(2,1)} %get-tuple-element.114.refs_2_.cotf_ref, ...), custom_call_target="tpu_custom_call" | custom-call | flops 345000000 | tf_op jit(solution)/shard_map/ffn_grad_two/pallas_call | solution.py:106
  226.4 4.7 %all-to-all-done.3.refs_1_ = f32[16,8,352]{2,1,0:T(8,128)S(1)} async-done(((f32[16,8,352]{2,1,0:T(8,128)}), f32[16,8,352]{2,1,0:T(8,128)S(1)}, u32[]{:S(2)}, u32[]{:S(2)}) %all-to-all-start.3) | async-done | bytes 180256 | tf_op jit(solution)/shard_map/all_to_all | solution.py:473
  231.8 4.0 %gate_bwd.1 = (bf16[256,352]{1,0:T(8,128)(2,1)}, bf16[256,352]{1,0:T(8,128)(2,1)}, f32[256,352]{1,0:T(8,128)}, f32[2,8,352]{2,1,0:T(8,128)}, f32[8,352]{1,0:T(8,128)}) custom-call(s32[8]{0:T(128)} %concatenate.21.s_ref.refs_0_, f32[16,8,352]{2,1,0:T(8,128)} %copy-done.19, f32[256,352]{1,0:T(8,128)} %get-tuple-element.125.refs_2_, ...), custom_call_target="tpu_custom_call" | custom-call | flops 4485000192 | tf_op jit(solution)/shard_map/gate_bwd/pallas_call | solution.py:106
  237.1 2.8 collective-permute-start.27
  242.7 5.7 %conv_bwd.1 = (bf16[256,352]{1,0:T(8,128)(2,1)}, bf16[4,272,256]{2,1,0:T(8,128)(2,1)}, bf16[4,272,256]{2,1,0:T(8,128)(2,1)}, f32[8,352]{1,0:T(8,128)}) custom-call(s32[8]{0:T(128)} %concatenate.21.s_ref.refs_0_, f32[256,352]{1,0:T(8,128)} %get-tuple-element.139.dc_ref, f32[2,8,352]{2,1,0:T(8,128)} %copy-done.48, f32[288,352]{1,0:T(8,128)} %get-tuple-element.141.vb_ref, ...), custom_call_target="tpu_custom_call" | custom-call | flops 6554999808 | tf_op jit(solution)/shard_map/conv_bwd/pallas_call | solution.py:106
  250.6 7.3 %collective-permute-done.28.refs_6_.refs_11_ = bf16[576,512]{1,0:T(8,128)(2,1)S(1)} collective-permute-done((bf16[576,512]{1,0:T(8,128)(2,1)}, bf16[576,512]{1,0:T(8,128)(2,1)S(1)}, u32[]{:S(2)}, u32[]{:S(2)}) %collective-permute-start.28) | collective-permute-done | bytes 589856 | tf_op jit(solution)/shard_map/ppermute | solution.py:598
  260.4 3.7 %late_grad.1.refs_14_ = bf16[16,448,128]{2,1,0:T(8,128)(2,1)} custom-call(bf16[256,352]{1,0:T(8,128)(2,1)} %get-tuple-element.143.refs_0_, bf16[256,2048]{1,0:T(8,128)(2,1)} %get-tuple-element.137.refs_3_.refs_1_, bf16[256,352]{1,0:T(8,128)(2,1)} %get-tuple-element.128.refs_7_.refs_2_, bf16[256,352]{1,0:T(8,128)(2,1)} %get-tuple-element.144.refs_3_, ...), custom_call_target="tpu_custom_call" | custom-call | flops 345000000 | tf_op jit(solution)/shard_map/late_grad/pallas_call | solution.py:106
  264.1 4.9 %all-to-all-start.4 = ((bf16[16,448,128]{2,1,0:T(8,128)(2,1)}), bf16[16,448,128]{2,1,0:T(8,128)(2,1)S(1)}, u32[]{:S(2)}, u32[]{:S(2)}) async-start(bf16[16,448,128]{2,1,0:T(8,128)(2,1)} %late_grad.1.refs_14_), calls=%async_computation.5 | async-start | bytes 3670016 | tf_op jit(solution)/shard_map/all_to_all | solution.py:473
  270.8 6.3 %ffn_grad_three.1 = (f32[1152,128]{1,0:T(8,128)}, bf16[1152,128]{1,0:T(8,128)(2,1)}, bf16[1152,128]{1,0:T(8,128)(2,1)}, bf16[1152,128]{1,0:T(8,128)(2,1)}, f32[1...) custom-call(s32[8]{0:T(128)} %concatenate.21.s_ref.refs_0_, ...), custom_call_target="tpu_custom_call" | custom-call | flops 7245000192 | tf_op jit(solution)/shard_map/ffn_grad_three/pallas_call | solution.py:106
  279.2 2.7 collective-permute-start.36
  283.4 2.7 collective-permute-start.34
  290.2 2.2 collective-permute-done.33.low_ref
  292.4 3.0 collective-permute-start.39
  295.4 2.7 finish.1
  299.0 3.5 %all-to-all-start.5 = ((f32[16,24,128]{2,1,0:T(8,128)}), f32[16,24,128]{2,1,0:T(8,128)S(1)}, u32[]{:S(2)}, u32[]{:S(2)}) async-start(f32[16,24,128]{2,1,0:T(8,128)} %get-tuple-element.158.refs_8_), calls=%async_computation.6 | async-start | bytes 393216 | tf_op jit(solution)/shard_map/all_to_all | solution.py:473
  302.5 2.5 late_out.1
  305.0 3.2 collective-permute-start.40
  308.2 2.6 all-to-all-done.5.got_ref
  315.5 2.9 ffn_out.1
  (217 shorter events, 55.8 us)
Async XLA Ops:
  7.2 58.1 %all-gather.5.cloned.1.call-start = ((), (), s32[]{:S(2)}) async-start(), calls=%async_computation.10 | async-start | bytes 4595712 | tf_op jit(solution)/shard_map/all_gather | solution.py:707
  9.1 135.5 %all-gather.7.cloned.1.call-start = ((), (), s32[]{:S(2)}) async-start(), calls=%async_computation.11 | async-start | bytes 10027008 | tf_op jit(solution)/shard_map/all_gather | solution.py:708
  11.3 237.7 %reduce-scatter.3.cloned.1.call-start = ((), (), s32[]{:S(2)}) async-start(), calls=%async_computation.8 | async-start | bytes 1179648 | tf_op jit(solution)/shard_map/reduce_scatter | solution.py:801
  11.4 17.4 %collective-permute-start.7 = (bf16[256,256]{1,0:T(8,128)(2,1)S(1)}, bf16[256,256]{1,0:T(8,128)(2,1)S(1)}, u32[]{:S(2)}, u32[]{:S(2)}) collective-permute-start(bf16[256,256]{1,0:T(8,128)(2,1)S(1)} %bitcast.92), channel_id=1, source_target_pairs={{0,6},{1,7},{2,0},{3,1},{4,2},{5,3},{6,4},{7,5},{8,14},{9,15},{10,... | collective-permute-start | bytes 393224 | tf_op jit(solution)/shard_map/ppermute | solution.py:440
  15.6 13.2 %collective-permute-start.6 = (bf16[256,256]{1,0:T(8,128)(2,1)S(1)}, bf16[256,256]{1,0:T(8,128)(2,1)S(1)}, u32[]{:S(2)}, u32[]{:S(2)}) collective-permute-start(bf16[256,256]{1,0:T(8,128)(2,1)S(1)} %bitcast.93), channel_id=1, source_target_pairs={{0,2},{1,3},{2,4},{3,5},{4,6},{5,7},{6,0},{7,1},{8,10},{9,11},{10,... | collective-permute-start | bytes 393224 | tf_op jit(solution)/shard_map/ppermute | solution.py:440
  15.6 4.8 %collective-permute-start = (bf16[2,16,256]{2,1,0:T(8,128)(2,1)S(1)}, bf16[2,16,256]{2,1,0:T(8,128)(2,1)S(1)}, u32[]{:S(2)}, u32[]{:S(2)}) collective-permute-start(bf16[2,16,256]{2,1,0:T(8,128)(2,1)S(1)} %slice.41), channel_id=1, source_target_pairs={{0,8},{8,16},{16,24},{24,32},{32,40},{40,48},{48,56},{56,64},{64,7... | collective-permute-start | bytes 49160 | tf_op jit(solution)/shard_map/ppermute | solution.py:719
  20.5 6.5 %collective-permute-start.1 = (bf16[304,256]{1,0:T(8,128)(2,1)S(1)}, bf16[304,256]{1,0:T(8,128)(2,1)S(1)}, u32[]{:S(2)}, u32[]{:S(2)}) collective-permute-start(bf16[304,256]{1,0:T(8,128)(2,1)S(1)} %maximum_maximum_fusion), channel_id=1, source_target_pairs={{0,2},{1,3},{2,4},{3,5},{4,6},{5,7},{6,0},{7,1},{8,10},{9,11},{10,... | collective-permute-start | bytes 466952 | tf_op jit(solution)/shard_map/ppermute | solution.py:440
  20.6 6.4 %collective-permute-start.2 = (bf16[304,256]{1,0:T(8,128)(2,1)S(1)}, bf16[304,256]{1,0:T(8,128)(2,1)S(1)}, u32[]{:S(2)}, u32[]{:S(2)}) collective-permute-start(bf16[304,256]{1,0:T(8,128)(2,1)S(1)} %maximum_maximum_fusion), channel_id=1, source_target_pairs={{0,6},{1,7},{2,0},{3,1},{4,2},{5,3},{6,4},{7,5},{8,14},{9,15},{10,... | collective-permute-start | bytes 466952 | tf_op jit(solution)/shard_map/ppermute | solution.py:440
  27.1 6.6 %collective-permute-start.3 = (bf16[304,256]{1,0:T(8,128)(2,1)S(1)}, bf16[304,256]{1,0:T(8,128)(2,1)S(1)}, u32[]{:S(2)}, u32[]{:S(2)}) collective-permute-start(bf16[304,256]{1,0:T(8,128)(2,1)S(1)} %broadcast_select_fusion), channel_id=1, source_target_pairs={{0,2},{1,7},{2,4},{3,1},{4,6},{5,3},{6,0},{7,5},{8,10},{9,15},{10,... | collective-permute-start | bytes 466952 | tf_op jit(solution)/shard_map/ppermute | solution.py:449
  28.7 8.8 %collective-permute-start.4 = (bf16[3,304,256]{2,1,0:T(8,128)(2,1)S(1)}, bf16[3,304,256]{2,1,0:T(8,128)(2,1)S(1)}, u32[]{:S(2)}, u32[]{:S(2)}) collective-permute-start(bf16[3,304,256]{2,1,0:T(8,128)(2,1)S(1)} %pad_maximum_fusion.1.three), channel_id=1, source_target_pairs={{0,1},{1,0},{2,3},{3,2},{4,5},{5,4},{6,7},{7,6},{8,9},{9,8},{10,11... | collective-permute-start | bytes 1400840 | tf_op jit(solution)/shard_map/ppermute | solution.py:444
  28.8 8.6 %collective-permute-start.8 = (bf16[256,256]{1,0:T(8,128)(2,1)S(1)}, bf16[256,256]{1,0:T(8,128)(2,1)S(1)}, u32[]{:S(2)}, u32[]{:S(2)}) collective-permute-start(bf16[256,256]{1,0:T(8,128)(2,1)S(1)} %broadcast_select_fusion.2), channel_id=1, source_target_pairs={{0,2},{1,7},{2,4},{3,1},{4,6},{5,3},{6,0},{7,5},{8,10},{9,15},{10,... | collective-permute-start | bytes 393224 | tf_op jit(solution)/shard_map/ppermute | solution.py:449
  33.7 3.8 %collective-permute-start.5 = (bf16[304,256]{1,0:T(8,128)(2,1)S(1)}, bf16[304,256]{1,0:T(8,128)(2,1)S(1)}, u32[]{:S(2)}, u32[]{:S(2)}) collective-permute-start(bf16[304,256]{1,0:T(8,128)(2,1)S(1)} %collective-permute-done.3.far), channel_id=1, source_target_pairs={{0,1},{1,0},{2,3},{3,2},{4,5},{5,4},{6,7},{7,6},{8,9},{9,8},{10,11... | collective-permute-start | bytes 466952 | tf_op jit(solution)/shard_map/ppermute | solution.py:444
  33.7 8.7 %collective-permute-start.9 = (bf16[3,256,256]{2,1,0:T(8,128)(2,1)S(1)}, bf16[3,256,256]{2,1,0:T(8,128)(2,1)S(1)}, u32[]{:S(2)}, u32[]{:S(2)}) collective-permute-start(bf16[3,256,256]{2,1,0:T(8,128)(2,1)S(1)} %pad_maximum_fusion.2.refs_6_.c3_ref), channel_id=1, source_target_pairs={{0,1},{1,0},{2,3},{3,2},{4,5},{5,4},{6,7},{7,6},{8,9},{9,8},{10,11... | collective-permute-start | bytes 1179656 | tf_op jit(solution)/shard_map/ppermute | solution.py:444
  37.4 5.0 %collective-permute-start.10 = (bf16[256,256]{1,0:T(8,128)(2,1)S(1)}, bf16[256,256]{1,0:T(8,128)(2,1)S(1)}, u32[]{:S(2)}, u32[]{:S(2)}) collective-permute-start(bf16[256,256]{1,0:T(8,128)(2,1)S(1)} %collective-permute-done.8.refs_7_.cf_ref), channel_id=1, source_target_pairs={{0,1},{1,0},{2,3},{3,2},{4,5},{5,4},{6,7},{7,6},{8,9},{9,8},{10,11... | collective-permute-start | bytes 393224 | tf_op jit(solution)/shard_map/ppermute | solution.py:444
  94.1 2.1 collective-permute-start.11
  97.4 6.2 %collective-permute-start.12 = (bf16[256,256]{1,0:T(8,128)(2,1)S(1)}, bf16[256,256]{1,0:T(8,128)(2,1)S(1)}, u32[]{:S(2)}, u32[]{:S(2)}) collective-permute-start(bf16[256,256]{1,0:T(8,128)(2,1)S(1)} %fusion.18), channel_id=1, source_target_pairs={{0,2},{1,7},{2,4},{3,1},{4,6},{5,3},{6,0},{7,5},{8,10},{9,15},{10,... | collective-permute-start | bytes 393224 | tf_op jit(solution)/shard_map/ppermute | solution.py:449
  103.8 6.2 %collective-permute-start.13 = (bf16[256,256]{1,0:T(8,128)(2,1)S(1)}, bf16[256,256]{1,0:T(8,128)(2,1)S(1)}, u32[]{:S(2)}, u32[]{:S(2)}) collective-permute-start(bf16[256,256]{1,0:T(8,128)(2,1)S(1)} %get-tuple-element.187), channel_id=1, source_target_pairs={{0,2},{1,3},{2,4},{3,5},{4,6},{5,7},{6,0},{7,1},{8,10},{9,11},{10,... | collective-permute-start | bytes 393224 | tf_op jit(solution)/shard_map/ppermute | solution.py:440
  104.2 5.8 %collective-permute-start.14 = (bf16[256,256]{1,0:T(8,128)(2,1)S(1)}, bf16[256,256]{1,0:T(8,128)(2,1)S(1)}, u32[]{:S(2)}, u32[]{:S(2)}) collective-permute-start(bf16[256,256]{1,0:T(8,128)(2,1)S(1)} %get-tuple-element.188), channel_id=1, source_target_pairs={{0,6},{1,7},{2,0},{3,1},{4,2},{5,3},{6,4},{7,5},{8,14},{9,15},{10,... | collective-permute-start | bytes 393224 | tf_op jit(solution)/shard_map/ppermute | solution.py:440
  110.8 5.8 %collective-permute-start.16 = (bf16[256,256]{1,0:T(8,128)(2,1)S(1)}, bf16[256,256]{1,0:T(8,128)(2,1)S(1)}, u32[]{:S(2)}, u32[]{:S(2)}) collective-permute-start(bf16[256,256]{1,0:T(8,128)(2,1)S(1)} %get-tuple-element.183), channel_id=1, source_target_pairs={{0,6},{1,7},{2,0},{3,1},{4,2},{5,3},{6,4},{7,5},{8,14},{9,15},{10,... | collective-permute-start | bytes 393224 | tf_op jit(solution)/shard_map/ppermute | solution.py:440
  114.0 6.4 %collective-permute-start.15 = (bf16[256,256]{1,0:T(8,128)(2,1)S(1)}, bf16[256,256]{1,0:T(8,128)(2,1)S(1)}, u32[]{:S(2)}, u32[]{:S(2)}) collective-permute-start(bf16[256,256]{1,0:T(8,128)(2,1)S(1)} %get-tuple-element.183), channel_id=1, source_target_pairs={{0,2},{1,3},{2,4},{3,5},{4,6},{5,7},{6,0},{7,1},{8,10},{9,11},{10,... | collective-permute-start | bytes 393224 | tf_op jit(solution)/shard_map/ppermute | solution.py:440
  120.5 7.7 %collective-permute-start.18 = (bf16[3,256,256]{2,1,0:T(8,128)(2,1)S(1)}, bf16[3,256,256]{2,1,0:T(8,128)(2,1)S(1)}, u32[]{:S(2)}, u32[]{:S(2)}) collective-permute-start(bf16[3,256,256]{2,1,0:T(8,128)(2,1)S(1)} %pad_maximum_fusion.3.three), channel_id=1, source_target_pairs={{0,1},{1,0},{2,3},{3,2},{4,5},{5,4},{6,7},{7,6},{8,9},{9,8},{10,11... | collective-permute-start | bytes 1179656 | tf_op jit(solution)/shard_map/ppermute | solution.py:444
  120.6 6.2 %collective-permute-start.17 = (bf16[256,256]{1,0:T(8,128)(2,1)S(1)}, bf16[256,256]{1,0:T(8,128)(2,1)S(1)}, u32[]{:S(2)}, u32[]{:S(2)}) collective-permute-start(bf16[256,256]{1,0:T(8,128)(2,1)S(1)} %broadcast_select_fusion.1), channel_id=1, source_target_pairs={{0,2},{1,7},{2,4},{3,1},{4,6},{5,3},{6,0},{7,5},{8,10},{9,15},{10,... | collective-permute-start | bytes 393224 | tf_op jit(solution)/shard_map/ppermute | solution.py:449
  157.7 2.2 collective-permute-start.20
  160.9 16.6 %all-to-all-start.1 = ((bf16[4,272,256]{2,1,0:T(8,128)(2,1)}), bf16[4,272,256]{2,1,0:T(8,128)(2,1)}, u32[]{:S(2)}, u32[]{:S(2)}) async-start(bf16[4,272,256]{2,1,0:T(8,128)(2,1)} %add_convert_fusion.refs_6_), calls=%async_computation.2 | async-start | bytes 1114112 | tf_op jit(solution)/shard_map/all_to_all | solution.py:469
  165.3 147.7 %reduce-scatter.5.cloned.1.call-start = ((), (), s32[]{:S(2)}) async-start(), calls=%async_computation.9 | async-start | bytes 3063808 | tf_op jit(solution)/shard_map/reduce_scatter | solution.py:827
  170.5 31.3 %collective-permute-start.23 = (bf16[576,1024]{1,0:T(8,128)(2,1)}, bf16[576,1024]{1,0:T(8,128)(2,1)S(1)}, u32[]{:S(2)}, u32[]{:S(2)}) collective-permute-start(bf16[576,1024]{1,0:T(8,128)(2,1)} %get-tuple-element.131), channel_id=1, source_target_pairs={{0,96},{8,104},{16,112},{24,120},{32,64},{40,72},{48,80},{56,88},{... | collective-permute-start | bytes 3538952 | tf_op jit(solution)/shard_map/ppermute | solution.py:598
  173.2 28.7 %collective-permute-start.24 = (bf16[576,1024]{1,0:T(8,128)(2,1)}, bf16[576,1024]{1,0:T(8,128)(2,1)S(1)}, u32[]{:S(2)}, u32[]{:S(2)}) collective-permute-start(bf16[576,1024]{1,0:T(8,128)(2,1)} %get-tuple-element.132), channel_id=1, source_target_pairs={{0,8},{8,0},{16,24},{24,16},{32,40},{40,32},{48,56},{56,48},{64,72... | collective-permute-start | bytes 3538952 | tf_op jit(solution)/shard_map/ppermute | solution.py:598
  173.3 28.8 %collective-permute-start.25 = (bf16[576,1024]{1,0:T(8,128)(2,1)}, bf16[576,1024]{1,0:T(8,128)(2,1)S(1)}, u32[]{:S(2)}, u32[]{:S(2)}) collective-permute-start(bf16[576,1024]{1,0:T(8,128)(2,1)} %get-tuple-element.133), channel_id=1, source_target_pairs={{0,24},{8,16},{16,8},{24,0},{32,56},{40,48},{48,40},{56,32},{64,88... | collective-permute-start | bytes 3538952 | tf_op jit(solution)/shard_map/ppermute | solution.py:598
  175.1 27.3 %collective-permute-start.22 = (bf16[576,1024]{1,0:T(8,128)(2,1)}, bf16[576,1024]{1,0:T(8,128)(2,1)}, u32[]{:S(2)}, u32[]{:S(2)}) collective-permute-start(bf16[576,1024]{1,0:T(8,128)(2,1)} %get-tuple-element.118.refs_2_), channel_id=1, source_target_pairs={{0,32},{8,40},{16,48},{24,56},{32,0},{40,8},{48,16},{56,24},{64,96... | collective-permute-start | bytes 3538952 | tf_op jit(solution)/shard_map/ppermute | solution.py:598
  193.2 1.9 collective-permute-start.21
  208.0 23.1 %all-to-all-start.3 = ((f32[16,8,352]{2,1,0:T(8,128)}), f32[16,8,352]{2,1,0:T(8,128)S(1)}, u32[]{:S(2)}, u32[]{:S(2)}) async-start(f32[16,8,352]{2,1,0:T(8,128)} %get-tuple-element.124), calls=%async_computation.4 | async-start | bytes 393216 | tf_op jit(solution)/shard_map/all_to_all | solution.py:473
  235.8 6.3 %collective-permute-start.26 = (f32[2,8,352]{2,1,0:T(8,128)}, f32[2,8,352]{2,1,0:T(8,128)S(1)}, u32[]{:S(2)}, u32[]{:S(2)}) collective-permute-start(f32[2,8,352]{2,1,0:T(8,128)} %get-tuple-element.140), channel_id=1, source_target_pairs={{8,0},{16,8},{24,16},{32,24},{40,32},{48,40},{56,48},{64,56},{72,6... | collective-permute-start | bytes 67592 | tf_op jit(solution)/shard_map/ppermute | solution.py:835
  237.1 22.1 %collective-permute-start.27 = (bf16[576,512]{1,0:T(8,128)(2,1)S(1)}, bf16[576,512]{1,0:T(8,128)(2,1)S(1)}, u32[]{:S(2)}, u32[]{:S(2)}) collective-permute-start(bf16[576,512]{1,0:T(8,128)(2,1)S(1)} %copy-done.30), channel_id=1, source_target_pairs={{0,96},{8,104},{16,112},{24,120},{32,64},{40,72},{48,80},{56,88},{... | collective-permute-start | bytes 1769480 | tf_op jit(solution)/shard_map/ppermute | solution.py:598
  239.8 18.1 %collective-permute-start.28 = (bf16[576,512]{1,0:T(8,128)(2,1)}, bf16[576,512]{1,0:T(8,128)(2,1)S(1)}, u32[]{:S(2)}, u32[]{:S(2)}) collective-permute-start(bf16[576,512]{1,0:T(8,128)(2,1)} %get-tuple-element.146), channel_id=1, source_target_pairs={{0,32},{8,40},{16,48},{24,56},{32,0},{40,8},{48,16},{56,24},{64,96... | collective-permute-start | bytes 1769480 | tf_op jit(solution)/shard_map/ppermute | solution.py:598
  240.4 18.8 %collective-permute-start.29 = (bf16[576,512]{1,0:T(8,128)(2,1)}, bf16[576,512]{1,0:T(8,128)(2,1)S(1)}, u32[]{:S(2)}, u32[]{:S(2)}) collective-permute-start(bf16[576,512]{1,0:T(8,128)(2,1)} %get-tuple-element.147), channel_id=1, source_target_pairs={{0,24},{8,16},{16,8},{24,0},{32,56},{40,48},{48,40},{56,32},{64,88... | collective-permute-start | bytes 1769480 | tf_op jit(solution)/shard_map/ppermute | solution.py:598
  240.7 18.5 %collective-permute-start.30 = (bf16[576,512]{1,0:T(8,128)(2,1)}, bf16[576,512]{1,0:T(8,128)(2,1)S(1)}, u32[]{:S(2)}, u32[]{:S(2)}) collective-permute-start(bf16[576,512]{1,0:T(8,128)(2,1)} %get-tuple-element.148), channel_id=1, source_target_pairs={{0,8},{8,0},{16,24},{24,16},{32,40},{40,32},{48,56},{56,48},{64,72... | collective-permute-start | bytes 1769480 | tf_op jit(solution)/shard_map/ppermute | solution.py:598
  248.4 20.6 %collective-permute-start.31 = (bf16[4,272,256]{2,1,0:T(8,128)(2,1)}, bf16[4,272,256]{2,1,0:T(8,128)(2,1)}, u32[]{:S(2)}, u32[]{:S(2)}) collective-permute-start(bf16[4,272,256]{2,1,0:T(8,128)(2,1)} %get-tuple-element.150), channel_id=1, source_target_pairs={{0,1},{1,0},{2,3},{3,2},{4,5},{5,4},{6,7},{7,6},{8,9},{9,8},{10,11... | collective-permute-start | bytes 1671176 | tf_op jit(solution)/shard_map/ppermute | solution.py:444
  264.1 34.9 %all-to-all-start.4 = ((bf16[16,448,128]{2,1,0:T(8,128)(2,1)}), bf16[16,448,128]{2,1,0:T(8,128)(2,1)S(1)}, u32[]{:S(2)}, u32[]{:S(2)}) async-start(bf16[16,448,128]{2,1,0:T(8,128)(2,1)} %late_grad.1.refs_14_), calls=%async_computation.5 | async-start | bytes 3670016 | tf_op jit(solution)/shard_map/all_to_all | solution.py:473
  270.2 13.2 %collective-permute-start.32 = (bf16[272,256]{1,0:T(8,128)(2,1)S(1)}, bf16[272,256]{1,0:T(8,128)(2,1)S(1)}, u32[]{:S(2)}, u32[]{:S(2)}) collective-permute-start(bf16[272,256]{1,0:T(8,128)(2,1)S(1)} %fusion.17), channel_id=1, source_target_pairs={{0,2},{1,7},{2,4},{3,1},{4,6},{5,3},{6,0},{7,5},{8,10},{9,15},{10,... | collective-permute-start | bytes 417800 | tf_op jit(solution)/shard_map/ppermute | solution.py:449
  277.2 27.8 %collective-permute-start.35 = (bf16[1152,128]{1,0:T(8,128)(2,1)}, bf16[1152,128]{1,0:T(8,128)(2,1)S(1)}, u32[]{:S(2)}, u32[]{:S(2)}) collective-permute-start(bf16[1152,128]{1,0:T(8,128)(2,1)} %get-tuple-element.173), channel_id=1, source_target_pairs={{0,8},{8,16},{16,24},{24,0},{32,40},{40,48},{48,56},{56,32},{64,72... | collective-permute-start | bytes 884744 | tf_op jit(solution)/shard_map/ppermute | solution.py:436
  279.2 35.5 %collective-permute-start.36 = (bf16[1152,128]{1,0:T(8,128)(2,1)}, bf16[1152,128]{1,0:T(8,128)(2,1)S(1)}, u32[]{:S(2)}, u32[]{:S(2)}) collective-permute-start(bf16[1152,128]{1,0:T(8,128)(2,1)} %get-tuple-element.174), channel_id=1, source_target_pairs={{0,16},{8,24},{16,0},{24,8},{32,48},{40,56},{48,32},{56,40},{64,80... | collective-permute-start | bytes 884744 | tf_op jit(solution)/shard_map/ppermute | solution.py:436
  281.9 32.8 %collective-permute-start.37 = (bf16[1152,128]{1,0:T(8,128)(2,1)}, bf16[1152,128]{1,0:T(8,128)(2,1)}, u32[]{:S(2)}, u32[]{:S(2)}) collective-permute-start(bf16[1152,128]{1,0:T(8,128)(2,1)} %get-tuple-element.175), channel_id=1, source_target_pairs={{0,24},{8,0},{16,8},{24,16},{32,56},{40,32},{48,40},{56,48},{64,88... | collective-permute-start | bytes 884744 | tf_op jit(solution)/shard_map/ppermute | solution.py:436
  283.4 5.3 %collective-permute-start.34 = (bf16[272,256]{1,0:T(8,128)(2,1)S(1)}, bf16[272,256]{1,0:T(8,128)(2,1)S(1)}, u32[]{:S(2)}, u32[]{:S(2)}) collective-permute-start(bf16[272,256]{1,0:T(8,128)(2,1)S(1)} %get-tuple-element.185), channel_id=1, source_target_pairs={{0,6},{1,7},{2,0},{3,1},{4,2},{5,3},{6,4},{7,5},{8,14},{9,15},{10,... | collective-permute-start | bytes 417800 | tf_op jit(solution)/shard_map/ppermute | solution.py:440
  286.2 6.3 %collective-permute-start.33 = (bf16[272,256]{1,0:T(8,128)(2,1)S(1)}, bf16[272,256]{1,0:T(8,128)(2,1)S(1)}, u32[]{:S(2)}, u32[]{:S(2)}) collective-permute-start(bf16[272,256]{1,0:T(8,128)(2,1)S(1)} %get-tuple-element.186), channel_id=1, source_target_pairs={{0,2},{1,3},{2,4},{3,5},{4,6},{5,7},{6,0},{7,1},{8,10},{9,11},{10,... | collective-permute-start | bytes 417800 | tf_op jit(solution)/shard_map/ppermute | solution.py:440
  288.8 26.0 %collective-permute-start.38 = (bf16[1152,128]{1,0:T(8,128)(2,1)S(1)}, bf16[1152,128]{1,0:T(8,128)(2,1)}, u32[]{:S(2)}, u32[]{:S(2)}) collective-permute-start(bf16[1152,128]{1,0:T(8,128)(2,1)S(1)} %copy-done.36), channel_id=1, source_target_pairs={{0,32},{8,40},{16,48},{24,56},{32,64},{40,72},{48,80},{56,88},{64,... | collective-permute-start | bytes 884744 | tf_op jit(solution)/shard_map/ppermute | solution.py:436
  292.4 22.3 %collective-permute-start.39 = (bf16[1152,128]{1,0:T(8,128)(2,1)S(1)}, bf16[1152,128]{1,0:T(8,128)(2,1)}, u32[]{:S(2)}, u32[]{:S(2)}) collective-permute-start(bf16[1152,128]{1,0:T(8,128)(2,1)S(1)} %copy-done.35), channel_id=1, source_target_pairs={{0,64},{8,72},{16,80},{24,88},{32,96},{40,104},{48,112},{56,120},{... | collective-permute-start | bytes 884744 | tf_op jit(solution)/shard_map/ppermute | solution.py:436
  299.0 11.8 %all-to-all-start.5 = ((f32[16,24,128]{2,1,0:T(8,128)}), f32[16,24,128]{2,1,0:T(8,128)S(1)}, u32[]{:S(2)}, u32[]{:S(2)}) async-start(f32[16,24,128]{2,1,0:T(8,128)} %get-tuple-element.158.refs_8_), calls=%async_computation.6 | async-start | bytes 393216 | tf_op jit(solution)/shard_map/all_to_all | solution.py:473
  305.0 9.7 %collective-permute-start.40 = (bf16[1152,128]{1,0:T(8,128)(2,1)S(1)}, bf16[1152,128]{1,0:T(8,128)(2,1)S(1)}, u32[]{:S(2)}, u32[]{:S(2)}) collective-permute-start(bf16[1152,128]{1,0:T(8,128)(2,1)S(1)} %copy-done.34), channel_id=1, source_target_pairs={{0,96},{8,104},{16,112},{24,120},{32,0},{40,8},{48,16},{56,24},{64... | collective-permute-start | bytes 884744 | tf_op jit(solution)/shard_map/ppermute | solution.py:436
  (52 other events, 330.5 us)
Sparse Core Ops, SparseCore 0:
  10.8 54.4 all-gather.4
  67.4 77.1 all-gather.6
  157.9 36.0 reduce-scatter.2
  208.1 87.9 reduce-scatter.4
